TPU v7x, 32 devices: a whole 2x2x4 slice. The times are simulated.
32 devices in a mesh: rep: 8 (over z, y), exp: 4 (over x, core).
Axes of the slice: x: 2, y: 2, z: 4, core: 2. Of those that a mesh axis runs over, the one named last changes fastest.
Arguments:
- tokens: bfloat16 [4096, 2048], P(('rep', 'exp')), may hold values from -6 to 6
- attend_weight: bfloat16 [2048, 16, 256], P(None, 'exp'), may hold values from -0.125 to 0.125
- value_weight: bfloat16 [2048, 32, 256], P(None, 'exp'), may hold values from -0.125 to 0.125
- rate_weight: bfloat16 [2048, 32, 2], P(None, 'exp'), may hold values from -0.125 to 0.125
- decay_rate: float32 [32], P('exp'), may hold values from 0.002 to 0.2
- output_weight: bfloat16 [32, 128, 2048], P('exp'), may hold values from -0.09375 to 0.09375
- state_cache: float32 [64, 32, 128, 128], P('rep', 'exp'), may hold values from -2.4 to 2.4
- resume_from: int32 [64], replicated, may hold values from 0 to 63, as said below
- expert_index: int32 [4096, 2], P(('rep', 'exp')), may hold values from 0 to 3, all different within a row; in each aligned block of 128 rows (0 to 127, 128 to 255, ...) at most 128 rows name the same one
- route_weight: float32 [4096, 2], P(('rep', 'exp')), may hold values from 0.02 to 0.3
- expert_inner: bfloat16 [4, 2048, 1024], P('exp'), may hold values from -0.125 to 0.125
- expert_outer: bfloat16 [4, 512, 2048], P('exp'), may hold values from -0.25 to 0.25
Outputs:
- layer_output: bfloat16 [4096, 2048], P(('rep', 'exp'))
- final_state: float32 [64, 32, 128, 128], P('rep', 'exp')
Inputs may be any that keep to these rules, and one draw needn't show every extreme that they name: `resume_from`: entry r * 8 + b is the cache row of trajectory b of group r; cache row c belongs to group c // 8. The 8 trajectories of one group take their rows from 8 different groups; a row may serve several groups. `expert_index`: each row names 2 different experts.
All inputs are finite; a program needn't handle non-finite values.
Results may differ from a plain program's by a relative error of at most 0.013.
Values may be sent and summed in bfloat16 or wider, within the bound.
A program may use at most 128 MiB of HBM per device.

v0:
```python
from functools import partial

import jax
import jax.numpy as jnp
from jax import lax
from jax.sharding import PartitionSpec as P

EPSILON = 1e-06
HIGHEST = lax.Precision.HIGHEST


def rms_scale(values):
    return values * lax.rsqrt(jnp.mean(values * values, axis=-1, keepdims=True) + EPSILON)


def unit_length(values):
    return values * lax.rsqrt(jnp.sum(values * values, axis=-1, keepdims=True) + EPSILON)


def head_inputs(attend_part, value_part, rate_part, key_heads, value_heads, decay_rate):
    count = attend_part.shape[0]
    key_size = attend_part.shape[1] // (2 * key_heads)
    value_size = value_part.shape[1] // (2 * value_heads)
    paired = attend_part.reshape(count, key_heads, 2, key_size)
    repeat = value_heads // key_heads
    query = jnp.repeat(unit_length(paired[:, :, 0]), repeat, axis=1) * key_size ** (-0.5)
    key_rows = jnp.repeat(unit_length(paired[:, :, 1]), repeat, axis=1)
    value_pair = value_part.reshape(count, value_heads, 2, value_size)
    rate_pair = rate_part.reshape(count, value_heads, 2)
    beta_rows = jax.nn.sigmoid(rate_pair[:, :, 1])
    log_decay = -decay_rate[None, :] * jax.nn.softplus(rate_pair[:, :, 0])
    return (query, key_rows, value_pair[:, :, 0], value_pair[:, :, 1], beta_rows, log_decay)


def block_step(state, packed):
    query, key_rows, value_rows, beta_rows, log_decay = packed
    summed = jnp.cumsum(log_decay, axis=-1)
    width = summed.shape[-1]
    row_iota = lax.broadcasted_iota(jnp.int32, (width, width), 0)
    col_iota = lax.broadcasted_iota(jnp.int32, (width, width), 1)
    spread = summed[..., :, None] - summed[..., None, :]
    ratio = jnp.where(col_iota <= row_iota, jnp.exp(jnp.minimum(spread, 0.0)), 0.0)
    key_products = jnp.einsum("bhik,bhjk->bhij", key_rows, key_rows, precision=HIGHEST)
    below = jnp.where(col_iota < row_iota, beta_rows[..., :, None] * ratio * key_products, 0.0)
    system = below + jnp.eye(width, dtype=jnp.float32)
    carried = jnp.einsum("bhik,bhvk->bhiv", key_rows, state, precision=HIGHEST)
    right_side = beta_rows[..., None] * (value_rows - jnp.exp(summed)[..., None] * carried)
    solver = jax.vmap(partial(jax.scipy.linalg.solve_triangular, lower=True, unit_diagonal=True))
    updates = solver(
        system.reshape(-1, width, width), right_side.reshape(-1, width, right_side.shape[-1])
    ).reshape(right_side.shape)
    query_keys = jnp.einsum("bhik,bhjk->bhij", query, key_rows, precision=HIGHEST)
    readout = jnp.exp(summed)[..., None] * jnp.einsum(
        "bhik,bhvk->bhiv", query, state, precision=HIGHEST
    )
    readout = readout + jnp.einsum(
        "bhij,bhjv->bhiv", ratio * query_keys, updates, precision=HIGHEST
    )
    closing = summed[..., -1:]
    tail = jnp.exp(closing - summed)
    new_state = jnp.exp(closing)[..., None] * state + jnp.einsum(
        "bhjv,bhjk->bhvk", updates * tail[..., None], key_rows, precision=HIGHEST
    )
    return (new_state, readout)


def local(
    tokens,
    attend_weight,
    value_weight,
    rate_weight,
    decay_rate,
    output_weight,
    state_cache,
    resume_from,
    expert_index,
    route_weight,
    expert_inner,
    expert_outer,
):
    model = tokens.shape[1]
    key_heads = attend_weight.shape[1]
    value_heads = value_weight.shape[1]
    attend_flat = attend_weight.reshape(model, -1)
    value_flat = value_weight.reshape(model, -1)
    rate_flat = rate_weight.reshape(model, -1)
    residual = tokens.astype(jnp.float32)
    normed = rms_scale(residual).astype(jnp.bfloat16)
    piece = lax.all_gather(normed, "exp", axis=0, tiled=True)
    projected = jnp.concatenate(
        [
            jnp.dot(piece, attend_flat, preferred_element_type=jnp.float32),
            jnp.dot(piece, value_flat, preferred_element_type=jnp.float32),
            jnp.dot(piece, rate_flat, preferred_element_type=jnp.float32),
        ],
        axis=1,
    )
    first_cut = attend_flat.shape[1]
    second_cut = first_cut + value_flat.shape[1]
    query, key_rows, value_rows, gate_rows, beta_rows, log_decay = head_inputs(
        projected[:, :first_cut],
        projected[:, first_cut:second_cut],
        projected[:, second_cut:],
        key_heads,
        value_heads,
        decay_rate,
    )
    trajs = state_cache.shape[0]
    replicas = lax.axis_size("rep")
    myself = lax.axis_index("rep")
    my_rows = lax.dynamic_slice_in_dim(resume_from, myself * trajs, trajs)
    listing = resume_from.reshape(replicas, trajs)
    from_me = listing // trajs == myself
    slot_pick = jnp.sum(jnp.where(from_me, listing % trajs, 0), axis=1)
    used = jnp.any(from_me, axis=1).astype(jnp.float32)
    outgoing = jnp.take(state_cache, slot_pick, axis=0) * used[:, None, None, None]
    incoming = lax.all_to_all(
        outgoing.astype(jnp.bfloat16), "rep", split_axis=0, concat_axis=0, tiled=True
    ).astype(outgoing.dtype)
    start = jnp.take(incoming, my_rows // trajs, axis=0)
    length = projected.shape[0] // trajs
    block = min(64, length)
    blocks = length // block

    def arrange(values):
        shaped = values.reshape((trajs, blocks, block) + values.shape[1:])
        return jnp.moveaxis(jnp.moveaxis(shaped, 3, 1), 2, 0)

    final_state, readout = lax.scan(
        block_step,
        start,
        (
            arrange(query),
            arrange(key_rows),
            arrange(value_rows),
            arrange(beta_rows),
            arrange(log_decay),
        ),
    )
    readout = jnp.transpose(readout, (1, 0, 3, 2, 4)).reshape(value_rows.shape)
    gated = (
        (rms_scale(readout) * jax.nn.silu(gate_rows))
        .astype(jnp.bfloat16)
        .reshape(readout.shape[0], -1)
    )
    output_flat = output_weight.reshape(-1, model)
    row_count = tokens.shape[0]
    attended = lax.psum_scatter(
        jnp.dot(gated, output_flat, preferred_element_type=jnp.float32).astype(jnp.bfloat16),
        "exp",
        scatter_dimension=0,
        tiled=True,
    ).astype(jnp.float32)
    hidden = residual + attended
    hidden_normed = rms_scale(hidden).astype(jnp.bfloat16)
    top_count = expert_index.shape[1]
    local_experts = expert_inner.shape[0]
    total_experts = lax.axis_size("exp") * local_experts
    flat_index = expert_index.reshape(-1)
    one_hot = (flat_index[:, None] == jnp.arange(total_experts, dtype=jnp.int32)[None, :]).astype(
        jnp.int32
    )
    earlier = jnp.cumsum(one_hot, axis=0) - one_hot
    slot_of_pair = jnp.sum(earlier * one_hot, axis=1)
    position = flat_index * row_count + slot_of_pair
    owner = jnp.arange(row_count * top_count, dtype=jnp.int32) // top_count
    table = jnp.full((total_experts * row_count,), row_count, jnp.int32).at[position].set(owner)
    padded = jnp.concatenate([hidden_normed, jnp.zeros((1, model), jnp.bfloat16)], axis=0)
    outgoing_rows = jnp.take(padded, table, axis=0).reshape(
        lax.axis_size("exp"), local_experts, row_count, model
    )
    inner = expert_outer.shape[1]
    both_parts = jnp.einsum(
        "semd,edf->semf",
        lax.all_to_all(outgoing_rows, "exp", split_axis=0, concat_axis=0, tiled=True),
        expert_inner,
        preferred_element_type=jnp.float32,
    )
    activated = (jax.nn.silu(both_parts[..., :inner]) * both_parts[..., inner:]).astype(
        jnp.bfloat16
    )
    produced = jnp.einsum(
        "semf,efd->semd", activated, expert_outer, preferred_element_type=jnp.float32
    ).astype(jnp.bfloat16)
    returned = lax.all_to_all(produced, "exp", split_axis=0, concat_axis=0, tiled=True)
    pair_output = jnp.take(
        returned.reshape(total_experts * row_count, model), position, axis=0
    ).reshape(row_count, top_count, model)
    expert_sum = jnp.einsum(
        "rt,rtd->rd", route_weight, pair_output.astype(jnp.float32), precision=HIGHEST
    )
    layer_output = (hidden + expert_sum).astype(jnp.bfloat16)
    return (layer_output, final_state)


def solution(mesh):
    in_specs = (
        P(("rep", "exp"), None),
        P(None, "exp", None),
        P(None, "exp", None),
        P(None, "exp", None),
        P("exp"),
        P("exp", None, None),
        P("rep", "exp", None, None),
        P(),
        P(("rep", "exp"), None),
        P(("rep", "exp"), None),
        P("exp", None, None),
        P("exp", None, None),
    )
    out_specs = (P(("rep", "exp"), None), P("rep", "exp", None, None))
    return jax.shard_map(local, mesh=mesh, in_specs=in_specs, out_specs=out_specs, check_vma=False)
```

profile of v0, /device:TPU:0, one launch (start us, length us, event | category | flops | bytes accessed | tf_op | source)
XLA Modules:
  0.0 349.8 jit_solution(14807558559703537875)
XLA Ops:
  11.0 5.0 %gather_fusion.2 = f32[8,8,128,128]{3,2,1,0:T(8,128)} fusion(f32[8,8,128,128]{3,2,1,0:T(8,128)} %param.20, s32[1024]{0:T(1024)S(1)} %pad_clamp_fusion.3), kind=kCustom, calls=%fused_computation.clone | custom fusion | bytes 8388640 | tf_op jit(solution)/shard_map/jit(_take)/gather | solution.py:116
  16.0 4.2 %fusion.2 = bf16[8,8,128,128]{3,2,1,0:T(8,128)(2,1)} fusion(f32[8,8,128,128]{3,2,1,0:T(8,128)} %gather_fusion.2, f32[8]{0:T(128)S(1)} %convert_element_type.67, pred[8]{0:T(512)(128)(4,1)S(1)} %compare_and_fusion.1), kind=kLoop, calls=%fused_computation.9 | loop fusion | flops 3145728 | bytes 6291496 | tf_op jit(solution)/shard_map/convert_element_type | solution.py:118
  20.2 7.4 %all-to-all-start = ((bf16[8,8,128,128]{3,2,1,0:T(8,128)(2,1)}), bf16[8,8,128,128]{3,2,1,0:T(8,128)(2,1)}, u32[]{:S(2)}, u32[]{:S(2)}) async-start(bf16[8,8,128,128]{3,2,1,0:T(8,128)(2,1)} %fusion.2), calls=%async_computation | async-start | bytes 4194304 | tf_op jit(solution)/shard_map/all_to_all | solution.py:117
  27.6 5.3 %copy.163 = bf16[256,8,4,256]{3,1,2,0:T(8,128)(2,1)} copy(bf16[256,8,4,256]{3,2,1,0:T(4,128)(2,1)} %bitcast.167) | data formatting | bytes 8388608
  32.9 6.6 %copy.129 = bf16[1024,2048]{1,0:T(8,128)(2,1)} copy(bf16[1024,2048]{0,1:T(8,128)(2,1)} %bitcast.161) | data formatting | bytes 8388608 | tf_op jit(solution)/shard_map/dot_general | solution.py:92
  39.6 10.3 %copy.164 = bf16[256,8,8,256]{3,1,2,0:T(8,128)(2,1)} copy(bf16[256,8,8,256]{3,2,1,0:T(8,128)(2,1)} %bitcast.163) | data formatting | bytes 16777216
  49.9 12.3 %copy.140 = bf16[2048,2048]{1,0:T(8,128)(2,1)} copy(bf16[2048,2048]{0,1:T(8,128)(2,1)} %bitcast.152) | data formatting | bytes 16777216 | tf_op jit(solution)/shard_map/dot_general | solution.py:93
  62.5 5.2 %fusion.13 = f32[512,4,2,128]{0,3,2,1:T(8,128)S(1)} fusion(bf16[4,2,128,2048]{3,2,1,0:T(8,128)(2,1)} %bitcast.168, bf16[512,2048]{1,0:T(8,128)(2,1)} %all-gather.2.cloned.1.call-done), kind=kOutput, calls=%fused_computation.24 | convolution fusion | flops 2147483648 | bytes 8388608 | tf_op jit(solution)/shard_map/dot_general | solution.py:92
  75.5 4.8 %select_add_fusion.1 = f32[8,8,64,64]{3,2,1,0:T(8,128)} fusion(f32[8,8,64,128]{3,2,0,1:T(8,128)S(1)} %bitcast.153, f32[64,64]{1,0:T(8,128)S(1)} %fusion.67, f32[8,8,64]{2,1,0:T(8,128)S(1)} %copy.135, f32[8,8,64]{2,1,0:T(8,128)S(1)} %reduce_window_sum.27, pred[64,64]{1,0:T(8,128)(4,1)S(1)} %get-tuple-element.45, pred[64,64]{1,0:T(8,128)(4,1)S(1)} %get-tuple-element.46), kind=kOutput, calls=%fused_computation.37 | convolution fusion | flops 404488192 | bytes 3203072 | tf_op jit(solution)/shard_map/while/body/eval_jaxpr/bhik,bhjk->bhij/dot_general | solution.py:43
  80.3 3.3 copy.138
  83.6 4.4 %select_add_fusion = f32[64,1,64,64]{0,3,2,1:T(8,128)} fusion(f32[64,1,64,64]{0,3,2,1:T(8,128)} %copy.138, f32[64,64]{1,0:T(8,128)S(1)} %get-tuple-element.48, pred[64,64]{1,0:T(8,128)(4,1)S(1)} %get-tuple-element.47), kind=kLoop, calls=%fused_computation.36 | loop fusion | flops 524288 | bytes 2117632 | tf_op jit(solution)/shard_map/while/body/eval_jaxpr/vmap(jit(_solve_triangular))/triangular_solve | solution.py:49
  88.0 68.5 %custom-call.5 = f32[64,1,64,64]{0,2,3,1:T(8,128)} custom-call(f32[64,1,64,64]{0,3,2,1:T(8,128)} %select_add_fusion), custom_call_target="InvertDiagBlocksLowerTriangular" | custom-call | tf_op jit(solution)/shard_map/while/body/eval_jaxpr/vmap(jit(_solve_triangular))/triangular_solve | solution.py:49
  156.5 4.1 %copy.144 = f32[64,64,64]{2,1,0:T(8,128)} copy(f32[64,64,64]{0,1,2:T(8,128)} %bitcast.171) | data formatting | bytes 2097152 | tf_op jit(solution)/shard_map/while/body/eval_jaxpr/vmap(jit(_solve_triangular))/triangular_solve | solution.py:49
  160.6 7.8 %fusion.11 = f32[512,8,2,128]{3,0,2,1:T(8,128)S(1)} fusion(bf16[8,2,128,2048]{3,2,1,0:T(8,128)(2,1)} %bitcast.164, bf16[512,2048]{1,0:T(8,128)(2,1)} %all-gather.2.cloned.1.call-done), kind=kOutput, calls=%fused_computation.22 | convolution fusion | flops 4294967296 | bytes 14680064 | tf_op jit(solution)/shard_map/dot_general | solution.py:93
  174.1 4.8 %fusion.26 = f32[8,8,64,64]{3,2,1,0:T(8,128)} fusion(f32[8,8,64,128]{3,2,0,1:T(8,128)S(1)} %bitcast.159, f32[8,8,64,128]{3,2,0,1:T(8,128)S(1)} %bitcast.155), kind=kOutput, calls=%fused_computation.45 | convolution fusion | flops 402653184 | bytes 5242880 | tf_op jit(solution)/shard_map/while/body/eval_jaxpr/bhik,bhjk->bhij/dot_general | solution.py:52
  178.9 4.1 %convert_element_type.69 = f32[8,8,128,128]{3,2,1,0:T(8,128)} convert(bf16[8,8,128,128]{3,2,1,0:T(8,128)(2,1)} %all-to-all-done) | non-fusion elementwise | flops 1048576 | bytes 6291456 | tf_op jit(solution)/shard_map/convert_element_type | solution.py:119
  183.0 4.9 %gather_fusion.3 = f32[8,8,128,128]{3,2,1,0:T(8,128)} fusion(f32[8,8,128,128]{3,2,1,0:T(8,128)} %convert_element_type.69, s32[1024]{0:T(1024)S(1)} %pad_clamp_fusion.2), kind=kCustom, calls=%fused_computation.1.clone | custom fusion | bytes 8388640 | tf_op jit(solution)/shard_map/jit(_take)/gather | solution.py:120
  187.9 11.4 %fusion.5 = f32[8,8,64,128]{3,2,1,0:T(8,128)S(1)} fusion(f32[8,8,128,128]{3,2,1,0:T(8,128)} %gather_fusion.3, pred[8]{0:T(512)(128)(4,1)S(1)} %get-tuple-element.23, f32[8,8,64,128]{3,2,0,1:T(8,128)} %bitcast.160), kind=kOutput, calls=%fused_computation.13 | convolution fusion | flops 806354944 | bytes 8388616 | tf_op jit(solution)/shard_map/while/body/eval_jaxpr/bhik,bhvk->bhiv/dot_general | solution.py:53
  199.4 8.4 %fusion.8 = f32[8,8,64,128]{3,2,1,0:T(8,128)S(1)} fusion(f32[8,1,64,8,128]{4,2,0,3,1:T(8,128)S(1)} %bitcast.166, f32[8,8,128,128]{3,2,1,0:T(8,128)S(1)} %copy-done.1, pred[8]{0:T(512)(128)(4,1)S(1)} %get-tuple-element.23, f32[8,8,64,128]{3,2,0,1:T(8,128)S(1)} %bitcast.156, f32[8,8,64]{2,1,0:T(8,128)S(1)} %copy.135, f32[8,8,64]{2,1,0:T(8,128)S(1)} %get-tuple-element.38), kind=kOutput, calls=%fused_computation.19 | convolution fusion | flops 807927808 | bytes 10518536 | tf_op jit(solution)/shard_map/while/body/eval_jaxpr/bhik,bhvk->bhiv/dot_general | solution.py:46
  210.1 3.7 %multiply_reduce_fusion = (f32[8,64,8]{1,2,0:T(8,128)S(1)}, f32[8,1,64,8,128]{4,2,3,0,1:T(8,128)S(1)}) fusion(f32[8,8,64,128]{3,2,1,0:T(8,128)S(1)} %bitcast.157, f32[8,8,64,64]{3,2,1,0:T(8,128)S(1)} %copy-done.8, f32[8,8,64]{2,1,0:T(8,128)S(1)} %reduce_window_sum.27, pred[64,64]{1,0:T(8,128)(4,1)S(1)} %get-tuple-element.46, ...), kind=kOutput, calls=%fused_computation.34 | convolution fusion | flops 405794816 | bytes 7393280 | tf_op jit(solution)/shard_map/while/body/eval_jaxpr/bhij,bhjv->bhiv/dot_general | solution.py:56
  213.8 2.7 copy.145
  216.6 7.3 %bitcast_convert_fusion = bf16[512,2048]{1,0:T(8,128)(2,1)} fusion(bf16[8,128,2048]{2,1,0:T(8,128)(2,1)} %param.19, f32[512,8,128]{2,1,0:T(8,128)} %bitcast.169, f32[512,8,2,128]{3,0,2,1:T(8,128)} %copy-done.10, f32[512,8]{0,1:T(8,128)S(1)} %rsqrt.47), kind=kOutput, calls=%fused_computation.7 | convolution fusion | flops 2152202240 | bytes 10502144 | tf_op jit(solution)/shard_map/dot_general | solution.py:149
  228.4 28.5 %reduce-scatter.2.cloned.1.call-done = bf16[128,2048]{1,0:T(8,128)(2,1)} async-done(((bf16[512,2048]{1,0:T(8,128)(2,1)}), bf16[128,2048]{1,0:T(8,128)(2,1)}) %reduce-scatter.2.cloned.1.call-update) | async-done | bytes 524304 | tf_op jit(solution)/shard_map/reduce_scatter | solution.py:148
  259.5 3.3 gather_fusion
  264.6 28.4 %all_to_all.15 = bf16[4,1,128,2048]{3,2,1,0:T(8,128)(2,1)S(1)} all-to-all(bf16[4,1,128,2048]{3,2,1,0:T(8,128)(2,1)S(1)} %broadcast_select_fusion), channel_id=1, replica_groups=mesh['rep'=8,'exp'=4] {'exp'}, dimensions={0} | all-to-all | bytes 4194304 | tf_op jit(solution)/shard_map/all_to_all | solution.py:175
  295.4 2.6 fusion.7
  298.0 4.8 %all-to-all-start.2 = ((bf16[4,1,128,2048]{3,2,1,0:T(8,128)(2,1)}), bf16[4,1,128,2048]{3,2,1,0:T(8,128)(2,1)}, u32[]{:S(2)}, u32[]{:S(2)}) async-start(bf16[4,1,128,2048]{3,2,1,0:T(8,128)(2,1)} %fusion.7), calls=%async_computation.3 | async-start | bytes 4194304 | tf_op jit(solution)/shard_map/all_to_all | solution.py:185
  303.3 13.5 %multiply_add_fusion = f32[8,8,128,128]{3,2,1,0:T(8,128)} fusion(f32[8,8,128,128]{3,2,1,0:T(8,128)} %gather_fusion.3, f32[8,8,64,128]{3,2,1,0:T(8,128)} %bitcast.158, f32[8,8]{1,0:T(8,128)S(1)} %get-tuple-element.22, pred[8]{0:T(512)(128)(4,1)S(1)} %get-tuple-element.23, f32[8,8,64,128]{3,2,0,1:T(8,128)} %bitcast.154, f32[8,8,64]{2,1,0:T(8,128)S(1)} %get-tuple-element.37), kind=kOutput, calls=%fused_computation.10 | convolution fusion | flops 808976384 | bytes 12599560 | tf_op jit(solution)/shard_map/while/body/eval_jaxpr/bhjv,bhjk->bhvk/dot_general | solution.py:61
  316.8 11.8 %all-to-all-done.2 = bf16[4,1,128,2048]{3,2,1,0:T(8,128)(2,1)} async-done(((bf16[4,1,128,2048]{3,2,1,0:T(8,128)(2,1)}), bf16[4,1,128,2048]{3,2,1,0:T(8,128)(2,1)}, u32[]{:S(2)}, u32[]{:S(2)}) %all-to-all-start.2) | async-done | bytes 2097184 | tf_op jit(solution)/shard_map/all_to_all | solution.py:185
  328.6 5.2 %gather_fusion.1 = bf16[256,2048]{1,0:T(8,128)(2,1)} fusion(bf16[512,2048]{1,0:T(8,128)(2,1)} %bitcast.61, s32[1024]{0:T(1024)S(1)} %pad_clamp_fusion), kind=kCustom, calls=%fused_computation.3 | custom fusion | bytes 2098176 | tf_op jit(solution)/shard_map/jit(_take)/gather | solution.py:186
  333.8 2.8 gather.18
  336.6 4.8 %fusion.59 = f32[128,1,2048]{2,1,0:T(1,128)S(1)} fusion(f32[128,2,1]{1,2,0:T(1,128)S(1)} %copy.159, bf16[128,2,2048]{2,1,0:T(2,128)(2,1)} %gather.18, pred[128,2]{1,0:T(8,128)(4,1)S(1)} %copy.153), kind=kOutput, calls=%fused_computation.77 | convolution fusion | flops 6815744 | bytes 2098432 | tf_op jit(solution)/shard_map/rt,rtd->rd/dot_general | solution.py:189
  (117 shorter events, 32.9 us)
Async XLA Ops:
  7.2 288.3 %copy-start = (bf16[1,512,2048]{2,1,0:T(8,128)(2,1)S(1)}, bf16[1,512,2048]{2,1,0:T(8,128)(2,1)}, u32[]{:S(2)}) copy-start(bf16[1,512,2048]{2,1,0:T(8,128)(2,1)} %param.25) | copy-start | bytes 6291460
  7.2 3.5 copy-start.14
  7.2 55.3 %all-gather.2.cloned.1.call-start = ((), (), s32[]{:S(2)}) async-start(), calls=%async_computation.4 | async-start | bytes 2621440 | tf_op jit(solution)/shard_map/all_gather | solution.py:89
  20.2 158.7 %all-to-all-start = ((bf16[8,8,128,128]{3,2,1,0:T(8,128)(2,1)}), bf16[8,8,128,128]{3,2,1,0:T(8,128)(2,1)}, u32[]{:S(2)}, u32[]{:S(2)}) async-start(bf16[8,8,128,128]{3,2,1,0:T(8,128)(2,1)} %fusion.2), calls=%async_computation | async-start | bytes 4194304 | tf_op jit(solution)/shard_map/all_to_all | solution.py:117
  27.6 229.3 %reduce-scatter.2.cloned.1.call-start = ((), (), s32[]{:S(2)}) async-start(), calls=%async_computation.5 | async-start | bytes 2621440 | tf_op jit(solution)/shard_map/reduce_scatter | solution.py:148
  32.9 6.7 %copy-start.12 = (bf16[2048,8,2]{0,2,1:T(2,128)(2,1)S(1)}, bf16[2048,8,2]{0,2,1:T(2,128)(2,1)}, u32[]{:S(2)}) copy-start(bf16[2048,8,2]{0,2,1:T(2,128)(2,1)} %param.17) | copy-start | bytes 196612
  32.9 6.7 %copy-start.17 = (f32[8]{0:T(128)S(1)}, f32[8]{0:T(128)}, u32[]{:S(2)}) copy-start(f32[8]{0:T(128)} %param.18) | copy-start | bytes 100
  75.5 4.8 %copy-start.2 = (f32[512,4,2,128]{3,0,2,1:T(8,128)}, f32[512,4,2,128]{3,0,2,1:T(8,128)S(1)}, u32[]{:S(2)}) copy-start(f32[512,4,2,128]{3,0,2,1:T(8,128)S(1)} %broadcast_in_dim.90) | copy-start | bytes 6291460
  168.4 2.0 copy-start.10
  172.0 2.1 copy-start.3
  172.4 1.3 copy-start.6
  187.9 11.4 %copy-start.1 = (f32[8,8,128,128]{3,2,1,0:T(8,128)S(1)}, f32[8,8,128,128]{3,2,1,0:T(8,128)}, u32[]{:S(2)}) copy-start(f32[8,8,128,128]{3,2,1,0:T(8,128)} %gather_fusion.3) | copy-start | bytes 12582916
  187.9 11.4 %copy-start.4 = (f32[512,4,2,128]{3,0,2,1:T(8,128)S(1)}, f32[512,4,2,128]{3,0,2,1:T(8,128)}, u32[]{:S(2)}) copy-start(f32[512,4,2,128]{3,0,2,1:T(8,128)} %copy-done.2) | copy-start | bytes 6291460
  187.9 11.4 %slice-start = ((f32[512,8,2,128]{3,0,2,1:T(8,128)}), f32[512,8,1,128]{3,0,2,1:T(8,128)S(1)}, s32[]{:S(2)}) async-start(f32[512,8,2,128]{3,0,2,1:T(8,128)} %copy-done.10), calls=%async_computation.6 | async-start | bytes 4194304 | tf_op jit(solution)/shard_map/slice | solution.py:32
  199.3 8.4 %copy-start.9 = (f32[64,64,64]{2,1,0:T(8,128)S(1)}, f32[64,64,64]{2,1,0:T(8,128)}, u32[]{:S(2)}) copy-start(f32[64,64,64]{2,1,0:T(8,128)} %copy.144) | copy-start | bytes 3145732
  207.7 2.3 copy-start.8
  210.0 3.8 %copy-start.5 = (f32[64,64,128]{2,1,0:T(8,128)}, f32[64,64,128]{2,1,0:T(8,128)S(1)}, u32[]{:S(2)}) copy-start(f32[64,64,128]{2,1,0:T(8,128)S(1)} %fusion.91) | copy-start | bytes 6291460
  223.9 0.7 copy-start.13
  223.9 32.9 %copy-start.7 = (bf16[128,2048]{1,0:T(8,128)(2,1)S(1)}, bf16[128,2048]{1,0:T(8,128)(2,1)}, u32[]{:S(2)}) copy-start(bf16[128,2048]{1,0:T(8,128)(2,1)} %param.14) | copy-start | bytes 1572868
  264.6 28.4 %copy-start.16 = (bf16[1,2048,1024]{2,1,0:T(8,128)(2,1)S(1)}, bf16[1,2048,1024]{2,1,0:T(8,128)(2,1)}, u32[]{:S(2)}) copy-start(bf16[1,2048,1024]{2,1,0:T(8,128)(2,1)} %param.24) | copy-start | bytes 12582916
  298.0 5.0 %copy-start.15 = (f32[128,2]{0,1:T(2,128)S(1)}, f32[128,2]{0,1:T(2,128)}, u32[]{:S(2)}) copy-start(f32[128,2]{0,1:T(2,128)} %param.23) | copy-start | bytes 3076
  298.0 30.6 %all-to-all-start.2 = ((bf16[4,1,128,2048]{3,2,1,0:T(8,128)(2,1)}), bf16[4,1,128,2048]{3,2,1,0:T(8,128)(2,1)}, u32[]{:S(2)}, u32[]{:S(2)}) async-start(bf16[4,1,128,2048]{3,2,1,0:T(8,128)(2,1)} %fusion.7), calls=%async_computation.3 | async-start | bytes 4194304 | tf_op jit(solution)/shard_map/all_to_all | solution.py:185
  336.6 4.8 %copy-start.11 = (bf16[128,2048]{1,0:T(8,128)(2,1)S(1)}, bf16[128,2048]{1,0:T(8,128)(2,1)}, u32[]{:S(2)}) copy-start(bf16[128,2048]{1,0:T(8,128)(2,1)} %reduce-scatter.2.cloned.1.call-done) | copy-start | bytes 1572868
Sparse Core Ops, SparseCore 0:
  10.7 25.2 all-gather.1
  224.1 32.7 reduce-scatter.1
where the time goes:
time: 354 us; the launch traced here: 350 us
  other arithmetic  95.8 us (27%)
  matrix products  81.1 us (23%)
  local copies, waits for them, and re-layouts  77 us (22%)
  waiting for transfers between devices  40.3 us (11%)
  blocking collectives  28.4 us (8%)
  between operations  14.8 us (4%)
  starting transfers between devices  12.2 us (3%)
    another operation x4, other arithmetic, block_step(): solver(system.reshape(-1, width, width), right_side.reshape(-1, width, ri...  72.9 us
    reduce_scatter x1, waiting for transfers between devices, local(): lax.psum_scatter(jnp.dot(gated, output_flat, preferred_element_type=jnp.f...  28.5 us
    all_to_all x1, blocking collectives, local(): lax.all_to_all(outgoing_rows, 'exp', split_axis=0, concat_axis=0, tiled=T...  28.4 us
    unnamed x40, local copies, waits for them, and re-layouts  20.2 us
    dot_general x1, matrix products, block_step(): jnp.einsum('bhjv,bhjk->bhvk', updates * tail[..., None], key_rows, precis...  13.5 us
    dot_general x1, local copies, waits for them, and re-layouts, local(): jnp.dot(piece, value_flat, preferred_element_type=jnp.float32)  12.3 us
    all_to_all x1, waiting for transfers between devices, local(): lax.all_to_all(produced, 'exp', split_axis=0, concat_axis=0, tiled=True)  11.8 us
    dot_general x1, matrix products, block_step(): jnp.einsum('bhik,bhvk->bhiv', query, state, precision=HIGHEST)  11.4 us
  transfers between devices with their start and end apart: 4, of which 2 were waited for; matrix products, arithmetic and copies ran while one was open for 50% of the time, Pallas kernels for 0%

commit v1 on v0

v1 whole, which is shorter than its diff:
```python
import jax
import jax.numpy as jnp
from jax import lax
from jax.experimental import pallas as pl
from jax.experimental.pallas import tpu as pltpu
from jax.sharding import PartitionSpec as P

EPSILON = 1e-06
HIGHEST = lax.Precision.HIGHEST
BF = jnp.bfloat16
F32 = jnp.float32


def rms_scale(values):
    return values * lax.rsqrt(jnp.mean(values * values, axis=-1, keepdims=True) + EPSILON)


def unit_length(values):
    return values * lax.rsqrt(jnp.sum(values * values, axis=-1, keepdims=True) + EPSILON)


def dot_nt(left, right):
    return lax.dot_general(
        left, right, (((1,), (1,)), ((), ())), preferred_element_type=F32
    )


def dot_tn(left, right):
    return lax.dot_general(
        left, right, (((0,), (0,)), ((), ())), preferred_element_type=F32
    )


def dot_nn(left, right):
    return jnp.dot(left, right, preferred_element_type=F32)


def pick_kernel(slot_ref, cache_ref, out_ref):
    out_ref[...] = cache_ref[...].astype(BF)


def pick_states(cache, slots):
    shape = cache.shape
    rows = slots.shape[0]
    block = (1,) + shape[1:]
    return pl.pallas_call(
        pick_kernel,
        grid_spec=pltpu.PrefetchScalarGridSpec(
            num_scalar_prefetch=1,
            grid=(rows,),
            in_specs=[pl.BlockSpec(block, lambda i, slot: (slot[i], 0, 0, 0))],
            out_specs=pl.BlockSpec(block, lambda i, slot: (i, 0, 0, 0)),
        ),
        out_shape=jax.ShapeDtypeStruct((rows,) + shape[1:], BF),
        compiler_params=pltpu.CompilerParams(vmem_limit_bytes=32 << 20),
    )(slots, cache)


def delta_kernel(source_ref, qk_ref, vz_ref, rate_ref, decay_ref, state_ref, gated_ref, final_ref):
    length = qk_ref.shape[0]
    value_heads, size, key_size = state_ref.shape[1:]
    key_heads = qk_ref.shape[1] // (2 * key_size)
    group = value_heads // key_heads
    wide = group * length
    rate = rate_ref[...]
    beta = jax.nn.sigmoid(rate)
    log_decay = -decay_ref[...] * jax.nn.softplus(rate)
    row = lax.broadcasted_iota(jnp.int32, (length, length), 0)
    col = lax.broadcasted_iota(jnp.int32, (length, length), 1)
    lower = (col <= row).astype(F32)
    summed = jnp.dot(lower, log_decay, precision=HIGHEST, preferred_element_type=F32)
    summed_rows = summed.T
    grow = jnp.exp(summed)
    closing = summed[length - 1 : length, :]
    tail = jnp.exp(closing - summed)
    close = jnp.exp(closing)

    wrow = lax.broadcasted_iota(jnp.int32, (wide, wide), 0)
    wcol = lax.broadcasted_iota(jnp.int32, (wide, wide), 1)
    same = wrow // length == wcol // length
    inclusive = same & (wcol <= wrow)
    strict = same & (wcol < wrow)
    eye = (wrow == wcol).astype(F32)

    def stack(values, at):
        return jnp.concatenate(
            [values[:, 2 * h + at : 2 * h + at + 1] for h in at_heads], axis=0
        )

    units = []
    for kh in range(key_heads):
        base = kh * 2 * key_size
        at_heads = range(kh * group, (kh + 1) * group)
        query = (unit_length(qk_ref[:, base : base + key_size]) * key_size ** (-0.5)).astype(BF)
        keys = unit_length(qk_ref[:, base + key_size : base + 2 * key_size]).astype(BF)
        both = jnp.concatenate([query] * group + [keys] * group, axis=0)
        keys_wide = both[wide:]
        products = dot_nt(both, keys_wide)
        states = state_ref[0, kh * group : (kh + 1) * group].reshape(group * size, key_size)
        carried = dot_nt(jnp.concatenate([query, keys], axis=0), states)
        cum_rows = jnp.concatenate([summed_rows[2 * h : 2 * h + 1, :] for h in at_heads], axis=1)
        spread = stack(summed, 0) - cum_rows
        ratio = jnp.where(inclusive, jnp.exp(jnp.minimum(spread, 0.0)), 0.0)
        beta_col = stack(beta, 1)
        grow_col = stack(grow, 0)
        below = jnp.where(strict, beta_col * ratio * products[wide:], 0.0)
        mixing = (ratio * products[:wide]).astype(BF)
        values = jnp.concatenate(
            [vz_ref[:, 2 * h * size : (2 * h + 1) * size] for h in at_heads], axis=0
        ).astype(F32)
        query_part = jnp.concatenate(
            [carried[:length, i * size : (i + 1) * size] for i in range(group)], axis=0
        )
        key_part = jnp.concatenate(
            [carried[length:, i * size : (i + 1) * size] for i in range(group)], axis=0
        )
        right_side = beta_col * (values - grow_col * key_part)
        units.append((keys, below, mixing, right_side, grow_col * query_part))

    inverses = []
    span = 1
    while span < length:
        corner = (wrow // (2 * span) == wcol // (2 * span)) & (
            (wrow // span) % 2 == 1
        ) & ((wcol // span) % 2 == 0)
        corners = [jnp.where(corner, unit[1], 0.0) for unit in units]
        if span == 1:
            inverses = [eye - c for c in corners]
        else:
            rounded = [t.astype(BF) for t in inverses]
            first = [dot_nn(c.astype(BF), t) for c, t in zip(corners, rounded)]
            inverses = [
                t - dot_nn(r, f.astype(BF)) for t, r, f in zip(inverses, rounded, first)
            ]
        span *= 2

    for kh in range(key_heads):
        keys, _, mixing, right_side, read = units[kh]
        updates = dot_nn(inverses[kh].astype(BF), right_side.astype(BF))
        readout = read + dot_nn(mixing, updates.astype(BF))
        scaled = rms_scale(readout)
        tailed = []
        for i in range(group):
            h = kh * group + i
            part = slice(i * length, (i + 1) * length)
            gate = vz_ref[:, (2 * h + 1) * size : (2 * h + 2) * size].astype(F32)
            gated_ref[:, h * size : (h + 1) * size] = (
                scaled[part] * jax.nn.silu(gate)
            ).astype(BF)
            tailed.append(updates[part] * tail[:, 2 * h : 2 * h + 1])
        added = dot_tn(jnp.concatenate(tailed, axis=1).astype(BF), keys)
        for i in range(group):
            h = kh * group + i
            final_ref[0, h] = (
                close[:, 2 * h : 2 * h + 1] * state_ref[0, h].astype(F32)
                + added[i * size : (i + 1) * size]
            )


def delta_rule(source, qk, vz, rate, decay_pairs, states):
    trajs = source.shape[0]
    length = qk.shape[0] // trajs
    heads, size, key_size = states.shape[1:]
    rows = lambda width: pl.BlockSpec((length, width), lambda i, s: (i, 0))
    return pl.pallas_call(
        delta_kernel,
        grid_spec=pltpu.PrefetchScalarGridSpec(
            num_scalar_prefetch=1,
            grid=(trajs,),
            in_specs=[
                rows(qk.shape[1]),
                rows(vz.shape[1]),
                rows(rate.shape[1]),
                pl.BlockSpec((1, rate.shape[1]), lambda i, s: (0, 0)),
                pl.BlockSpec((1, heads, size, key_size), lambda i, s: (s[i], 0, 0, 0)),
            ],
            out_specs=[
                rows(heads * size),
                pl.BlockSpec((1, heads, size, key_size), lambda i, s: (i, 0, 0, 0)),
            ],
        ),
        out_shape=[
            jax.ShapeDtypeStruct((qk.shape[0], heads * size), BF),
            jax.ShapeDtypeStruct((trajs, heads, size, key_size), F32),
        ],
        compiler_params=pltpu.CompilerParams(vmem_limit_bytes=48 << 20),
    )(source, qk, vz, rate, decay_pairs, states)


def local(
    tokens,
    attend_weight,
    value_weight,
    rate_weight,
    decay_rate,
    output_weight,
    state_cache,
    resume_from,
    expert_index,
    route_weight,
    expert_inner,
    expert_outer,
):
    model = tokens.shape[1]
    value_heads = value_weight.shape[1]
    residual = tokens.astype(F32)
    normed = rms_scale(residual).astype(BF)
    piece = lax.all_gather(normed, "exp", axis=0, tiled=True)

    trajs = state_cache.shape[0]
    replicas = lax.axis_size("rep")
    myself = lax.axis_index("rep")
    my_rows = lax.dynamic_slice_in_dim(resume_from, myself * trajs, trajs)
    listing = resume_from.reshape(replicas, trajs)
    from_me = listing // trajs == myself
    slot_pick = jnp.sum(jnp.where(from_me, listing % trajs, 0), axis=1)
    outgoing = pick_states(state_cache, slot_pick)
    incoming = lax.all_to_all(outgoing, "rep", split_axis=0, concat_axis=0, tiled=True)

    local_experts = expert_inner.shape[0]
    total_experts = lax.axis_size("exp") * local_experts
    numbers = jnp.arange(total_experts, dtype=jnp.int32)
    share = jnp.sum(
        jnp.where(expert_index[None] == numbers[:, None, None], route_weight[None], 0.0), axis=2
    )
    shares = lax.all_to_all(
        share.reshape(lax.axis_size("exp"), local_experts, -1),
        "exp", split_axis=0, concat_axis=0, tiled=True,
    )
    shares = jnp.moveaxis(shares, 1, 0).reshape(local_experts, -1)

    qk = jnp.dot(piece, attend_weight.reshape(model, -1), preferred_element_type=F32)
    vz = jnp.dot(piece, value_weight.reshape(model, -1), preferred_element_type=F32).astype(BF)
    rate = jnp.dot(piece, rate_weight.reshape(model, -1), preferred_element_type=F32)
    decay_pairs = jnp.repeat(decay_rate, 2)[None, :]
    gated, final_state = delta_rule(my_rows // trajs, qk, vz, rate, decay_pairs, incoming)

    output_flat = output_weight.reshape(-1, model)
    attended = lax.psum_scatter(
        jnp.dot(gated, output_flat, preferred_element_type=F32).astype(BF),
        "exp",
        scatter_dimension=0,
        tiled=True,
    ).astype(F32)
    hidden = residual + attended
    hidden_normed = rms_scale(hidden).astype(BF)
    everyone = lax.all_gather(hidden_normed, "exp", axis=0, tiled=True)
    inner = expert_outer.shape[1]
    weighted = 0.0
    for e in range(local_experts):
        both_parts = jnp.dot(everyone, expert_inner[e], preferred_element_type=F32)
        activated = (jax.nn.silu(both_parts[:, :inner]) * both_parts[:, inner:]).astype(BF)
        produced = jnp.dot(activated, expert_outer[e], preferred_element_type=F32)
        weighted = weighted + shares[e][:, None] * produced
    expert_sum = lax.psum_scatter(
        weighted.astype(BF), "exp", scatter_dimension=0, tiled=True
    ).astype(F32)
    layer_output = (hidden + expert_sum).astype(BF)
    return (layer_output, final_state)


def solution(mesh):
    in_specs = (
        P(("rep", "exp"), None),
        P(None, "exp", None),
        P(None, "exp", None),
        P(None, "exp", None),
        P("exp"),
        P("exp", None, None),
        P("rep", "exp", None, None),
        P(),
        P(("rep", "exp"), None),
        P(("rep", "exp"), None),
        P("exp", None, None),
        P("exp", None, None),
    )
    out_specs = (P(("rep", "exp"), None), P("rep", "exp", None, None))
    return jax.shard_map(local, mesh=mesh, in_specs=in_specs, out_specs=out_specs, check_vma=False)
```

time: 354 us -> 210 us (0.59); the launches traced: 350 us -> 210 us
  other arithmetic: 95.8 us -> 9.56 us
  waiting for transfers between devices: 40.3 us -> 101 us
  local copies, waits for them, and re-layouts: 77 us -> 20.6 us
  matrix products: 81.1 us -> 29.3 us
  blocking collectives: 28.4 us -> 0 us
  Pallas kernels: 0 us -> 25.3 us
    another operation x7 -> x0, other arithmetic: 76 us -> none  [the longest x4 72.9 us: block_step(): solver(system.reshape(-1, width, width), right_side.reshape(-1, width, ri...]
    dot_general x13 -> x6, matrix products: 78.9 us -> 29.3 us  [the longest x1 6.61 us: local(): jnp.dot(piece, attend_weight.reshape(model, -1), preferred_element_type=F32)]
    reduce_scatter x1 -> x2, waiting for transfers between devices: 28.5 us -> 62.2 us  [the longest x1 31.6 us: local(): lax.psum_scatter(weighted.astype(BF), 'exp', scatter_dimension=0, tiled=T...]
    all_to_all x1 -> x0, blocking collectives: 28.4 us -> none  [local(): lax.all_to_all(outgoing_rows, 'exp', split_axis=0, concat_axis=0, tiled=T...]
    pallas_call x0 -> x2, Pallas kernels: none -> 25.3 us  [the longest x1 24.4 us: delta_rule(): pl.pallas_call(delta_kernel, grid_spec=pltpu.PrefetchScalarGridSpec(num_s...]
    gather x5 -> x0, local copies, waits for them, and re-layouts: 21.2 us -> none  [the longest x2 7.98 us: local(): jnp.take(returned.reshape(total_experts * row_count, model), position, ax...]
    dot_general x3 -> x0, local copies, waits for them, and re-layouts: 19 us -> none  [the longest x1 12.3 us: local(): jnp.dot(piece, value_flat, preferred_element_type=jnp.float32)]
    all_gather x0 -> x1, waiting for transfers between devices: none -> 18.9 us  [local(): everyone = lax.all_gather(hidden_normed, 'exp', axis=0, tiled=True)]
  transfers between devices with their start and end apart: 4 -> 6, of which waited for: 2 -> 4; matrix products, arithmetic and copies ran while one was open for 50% -> 17% of each run, Pallas kernels for 0% -> 0%
where the time goes in v1:
time: 210 us
  waiting for transfers between devices  101 us (48%)
  matrix products  29.3 us (14%)
  Pallas kernels  25.3 us (12%)
  local copies, waits for them, and re-layouts  20.6 us (10%)
  between operations  13.9 us (7%)
  starting transfers between devices  10.6 us (5%)
  other arithmetic  9.56 us (5%)
    reduce_scatter x1, waiting for transfers between devices, local(): lax.psum_scatter(weighted.astype(BF), 'exp', scatter_dimension=0, tiled=T...  31.6 us
    reduce_scatter x1, waiting for transfers between devices, local(): lax.psum_scatter(jnp.dot(gated, output_flat, preferred_element_type=F32)....  30.6 us
    pallas_call x1, Pallas kernels, delta_rule(): pl.pallas_call(delta_kernel, grid_spec=pltpu.PrefetchScalarGridSpec(num_s...  24.4 us
    unnamed x36, local copies, waits for them, and re-layouts  20.3 us
    all_to_all x1, waiting for transfers between devices, local(): lax.all_to_all(outgoing, 'rep', split_axis=0, concat_axis=0, tiled=True)  19.5 us
    all_gather x1, waiting for transfers between devices, local(): everyone = lax.all_gather(hidden_normed, 'exp', axis=0, tiled=True)  18.9 us
    all_to_all x1, starting transfers between devices, local(): lax.all_to_all(outgoing, 'rep', split_axis=0, concat_axis=0, tiled=True)  7.28 us
    dot_general x1, matrix products, local(): jnp.dot(piece, attend_weight.reshape(model, -1), preferred_element_type=F32)  6.61 us
  transfers between devices with their start and end apart: 6, of which 4 were waited for; matrix products, arithmetic and copies ran while one was open for 17% of the time, Pallas kernels for 0%

profile of v1, /device:TPU:0, one launch (start us, length us, event | category | flops | bytes accessed | tf_op | source)
XLA Modules:
  0.0 209.8 jit_solution(11909408959532642140)
XLA Ops:
  7.2 1.4 fusion.3
  8.6 2.0 fusion.4
  10.6 0.1 reshape.44
  10.7 0.1 fusion.10.slot_ref
  10.9 2.2 %copy-done.2 = f32[8,8,128,128]{3,2,1,0:T(8,128)S(1)} copy-done((f32[8,8,128,128]{3,2,1,0:T(8,128)S(1)}, f32[8,8,128,128]{3,2,1,0:T(8,128)}, u32[]{:S(2)}) %copy-start.2) | copy-done | bytes 4194328
  13.0 0.9 shard_map.131
  13.9 1.3 copy-done.1
  15.3 7.3 %all-to-all-start = ((bf16[8,8,128,128]{3,2,1,0:T(8,128)(2,1)}), bf16[8,8,128,128]{3,2,1,0:T(8,128)(2,1)}, u32[]{:S(2)}, u32[]{:S(2)}) async-start(bf16[8,8,128,128]{3,2,1,0:T(8,128)(2,1)} %copy-done.1), calls=%async_computation | async-start | bytes 4194304 | tf_op jit(solution)/shard_map/all_to_all | solution.py:218
  22.6 10.5 %copy.27 = bf16[256,8,8,256]{3,1,2,0:T(8,128)(2,1)} copy(bf16[256,8,8,256]{3,2,1,0:T(8,128)(2,1)} %bitcast.26) | data formatting | bytes 16777216
  33.1 3.1 %copy.26 = bf16[256,8,4,256]{3,1,2,0:T(8,128)(2,1)} copy(bf16[256,8,4,256]{3,2,1,0:T(4,128)(2,1)S(1)} %bitcast.30) | data formatting | bytes 8388608
  36.2 0.1 broadcast_in_dim.22
  36.3 0.1 broadcast_in_dim_reshape.3.decay_ref
  36.4 0.1 and_select_fusion.source_ref
  36.4 2.4 %fusion.15.rate_ref = f32[512,16]{1,0:T(8,128)S(1)} fusion(bf16[512,2048]{1,0:T(8,128)(2,1)} %all-gather.3.cloned.1.call-done, bf16[2048,16]{0,1:T(8,128)(2,1)S(1)} %reshape.43), kind=kOutput, calls=%fused_computation.38 | convolution fusion | flops 33554432 | bytes 2195456 | tf_op jit(solution)/shard_map/dot_general | solution.py:234
  38.9 6.6 %fusion.14.qk_ref = f32[512,1024]{1,0:T(8,128)} fusion(bf16[512,2048]{1,0:T(8,128)(2,1)} %all-gather.3.cloned.1.call-done, bf16[2048,1024]{1,0:T(8,128)(2,1)} %bitcast.31), kind=kOutput, calls=%fused_computation.37 | convolution fusion | flops 2147483648 | bytes 8388608 | tf_op jit(solution)/shard_map/dot_general | solution.py:232
  45.5 5.9 %convolution_convert_fusion.1.vz_ref = bf16[512,2048]{1,0:T(8,128)(2,1)} fusion(bf16[512,2048]{1,0:T(8,128)(2,1)S(1)} %copy-done.14, bf16[2048,2048]{1,0:T(8,128)(2,1)S(1)} %bitcast.29), kind=kOutput, calls=%fused_computation.4 | convolution fusion | flops 4296015872 | bytes 12582912 | tf_op jit(solution)/shard_map/dot_general | solution.py:233
  51.4 19.5 %all-to-all-done.state_ref = bf16[8,8,128,128]{3,2,1,0:T(8,128)(2,1)} async-done(((bf16[8,8,128,128]{3,2,1,0:T(8,128)(2,1)}), bf16[8,8,128,128]{3,2,1,0:T(8,128)(2,1)}, u32[]{:S(2)}, u32[]{:S(2)}) %all-to-all-start) | async-done | bytes 2097184 | tf_op jit(solution)/shard_map/all_to_all | solution.py:218
  70.9 1.6 copy-done.3
  72.5 1.6 copy-done.4
  74.1 24.4 %shard_map.132 = (bf16[512,1024]{1,0:T(8,128)(2,1)S(1)}, f32[8,8,128,128]{3,2,1,0:T(8,128)}) custom-call(s32[8]{0:T(128)S(1)} %and_select_fusion.source_ref, f32[512,1024]{1,0:T(8,128)S(1)} %copy-done.3, bf16[512,2048]{1,0:T(8,128)(2,1)S(1)} %copy-done.4, f32[512,16]{1,0:T(8,128)S(1)} %fusion.15.rate_ref, f32[1,16]{1,0:T(1,128)S(1)} %broadcast_in_dim_reshape.3.decay_ref, ...), custom_call_target="tpu_custom_call" | custom-call | tf_op jit(solution)/shard_map/pallas_call | solution.py:165
  98.5 3.7 %convolution_convert_fusion = bf16[512,2048]{1,0:T(8,128)(2,1)} fusion(bf16[512,1024]{1,0:T(8,128)(2,1)S(1)} %get-tuple-element.4, bf16[1024,2048]{1,0:T(8,128)(2,1)S(1)} %bitcast.33), kind=kOutput, calls=%fused_computation.3 | convolution fusion | flops 2148532224 | bytes 7340032 | tf_op jit(solution)/shard_map/dot_general | solution.py:240
  102.2 30.6 %reduce-scatter.3.cloned.1.call-done = bf16[128,2048]{1,0:T(8,128)(2,1)} async-done(((bf16[512,2048]{1,0:T(8,128)(2,1)}), bf16[128,2048]{1,0:T(8,128)(2,1)}) %reduce-scatter.3.cloned.1.call-update) | async-done | bytes 524304 | tf_op jit(solution)/shard_map/reduce_scatter | solution.py:239
  132.8 1.3 multiply_reduce_fusion
  134.1 2.0 multiply_convert_fusion.1
  136.2 0.6 select_reduce_fusion
  136.8 3.2 %all-to-all-start.1 = ((f32[4,1,128]{2,1,0:T(1,128)}), f32[4,1,128]{2,1,0:T(1,128)S(1)}, u32[]{:S(2)}, u32[]{:S(2)}) async-start(f32[4,1,128]{2,1,0:T(1,128)} %bitcast.2), calls=%async_computation.2 | async-start | bytes 4096 | tf_op jit(solution)/shard_map/all_to_all | solution.py:226
  139.9 0.0 reduce-scatter.5.cloned.1.call-start
  140.0 18.9 %all-gather.5.cloned.1.call-done = bf16[512,2048]{1,0:T(8,128)(2,1)} async-done(((bf16[128,2048]{1,0:T(8,128)(2,1)}), bf16[512,2048]{1,0:T(8,128)(2,1)}) %all-gather.5.cloned.1.call-update) | async-done | bytes 2097168 | tf_op jit(solution)/shard_map/all_gather | solution.py:247
  158.9 6.5 %fusion = f32[512,1024]{1,0:T(8,128)} fusion(bf16[512,2048]{1,0:T(8,128)(2,1)} %all-gather.5.cloned.1.call-done, bf16[1,2048,1024]{2,1,0:T(8,128)(2,1)} %param.22), kind=kOutput, calls=%fused_computation | convolution fusion | flops 2147483648 | bytes 8388608 | tf_op jit(solution)/shard_map/dot_general | solution.py:251
  165.4 4.2 %multiply_convert_fusion = bf16[512,2048]{1,0:T(8,128)(2,1)} fusion(bf16[1,512,2048]{2,1,0:T(8,128)(2,1)S(1)} %copy-done, f32[512]{0:T(512)S(1)} %bitcast.32, f32[512,1024]{1,0:T(8,128)} %fusion), kind=kOutput, calls=%fused_computation.2 | convolution fusion | flops 1077411840 | bytes 6293504 | tf_op jit(solution)/shard_map/dot_general | solution.py:253
  169.6 31.6 %reduce-scatter.5.cloned.1.call-done = bf16[128,2048]{1,0:T(8,128)(2,1)} async-done(((bf16[512,2048]{1,0:T(8,128)(2,1)}), bf16[128,2048]{1,0:T(8,128)(2,1)}) %reduce-scatter.5.cloned.1.call-update) | async-done | bytes 524304 | tf_op jit(solution)/shard_map/reduce_scatter | solution.py:255
  201.2 2.1 add_convert_fusion
  (43 shorter events, 0.3 us)
Async XLA Ops:
  7.2 158.2 %copy-start = (bf16[1,512,2048]{2,1,0:T(8,128)(2,1)S(1)}, bf16[1,512,2048]{2,1,0:T(8,128)(2,1)}, u32[]{:S(2)}) copy-start(bf16[1,512,2048]{2,1,0:T(8,128)(2,1)} %param.23) | copy-start | bytes 6291460
  7.2 3.5 %copy-start.12 = (s32[64]{0:T(128)S(1)}, s32[64]{0:T(128)}, u32[]{:S(2)}) copy-start(s32[64]{0:T(128)} %param.19) | copy-start | bytes 772
  7.2 29.2 %all-gather.3.cloned.1.call-start = ((), (), s32[]{:S(2)}) async-start(), calls=%async_computation.4 | async-start | bytes 2621440 | tf_op jit(solution)/shard_map/all_gather | solution.py:208
  10.8 2.2 %copy-start.2 = (f32[8,8,128,128]{3,2,1,0:T(8,128)S(1)}, f32[8,8,128,128]{3,2,1,0:T(8,128)}, u32[]{:S(2)}) copy-start(f32[8,8,128,128]{3,2,1,0:T(8,128)} %cache_ref.1) | copy-start | bytes 12582916
  13.9 1.3 copy-start.1
  15.3 55.6 %all-to-all-start = ((bf16[8,8,128,128]{3,2,1,0:T(8,128)(2,1)}), bf16[8,8,128,128]{3,2,1,0:T(8,128)(2,1)}, u32[]{:S(2)}, u32[]{:S(2)}) async-start(bf16[8,8,128,128]{3,2,1,0:T(8,128)(2,1)} %copy-done.1), calls=%async_computation | async-start | bytes 4194304 | tf_op jit(solution)/shard_map/all_to_all | solution.py:218
  22.6 110.3 %reduce-scatter.3.cloned.1.call-start = ((), (), s32[]{:S(2)}) async-start(), calls=%async_computation.5 | async-start | bytes 2621440 | tf_op jit(solution)/shard_map/reduce_scatter | solution.py:239
  22.6 10.5 %copy-start.7 = (bf16[2048,4,256]{2,1,0:T(4,128)(2,1)S(1)}, bf16[2048,4,256]{2,1,0:T(4,128)(2,1)}, u32[]{:S(2)}) copy-start(bf16[2048,4,256]{2,1,0:T(4,128)(2,1)} %param.13) | copy-start | bytes 12582916
  33.1 3.1 %copy-start.8 = (bf16[2048,8,2]{0,2,1:T(2,128)(2,1)S(1)}, bf16[2048,8,2]{0,2,1:T(2,128)(2,1)}, u32[]{:S(2)}) copy-start(bf16[2048,8,2]{0,2,1:T(2,128)(2,1)} %param.15) | copy-start | bytes 196612
  33.1 3.1 %copy-start.11 = (f32[8]{0:T(128)S(1)}, f32[8]{0:T(128)}, u32[]{:S(2)}) copy-start(f32[8]{0:T(128)} %param.16) | copy-start | bytes 100
  36.4 9.1 %slice-start = ((s8[8388608]{0:T(1024)(128)(4,1)}), s8[4194304]{0:T(1024)(128)(4,1)S(1)}, s32[]{:S(2)}) async-start(s8[8388608]{0:T(1024)(128)(4,1)} %bitcast.27), calls=%async_computation.8 | async-start | bytes 8388608
  38.9 6.6 %slice-start.1 = ((s8[8388608]{0:T(1024)(128)(4,1)}), s8[4194304]{0:T(1024)(128)(4,1)S(1)}, s32[]{:S(2)}) async-start(s8[8388608]{0:T(1024)(128)(4,1)} %bitcast.27), calls=%async_computation.9 | async-start | bytes 8388608
  38.9 6.6 %copy-start.14 = (bf16[512,2048]{1,0:T(8,128)(2,1)S(1)}, bf16[512,2048]{1,0:T(8,128)(2,1)}, u32[]{:S(2)}) copy-start(bf16[512,2048]{1,0:T(8,128)(2,1)} %all-gather.3.cloned.1.call-done) | copy-start | bytes 6291460
  70.9 1.6 copy-start.3
  72.5 1.6 copy-start.4
  74.1 24.4 %copy-start.13 = (bf16[8,128,2048]{2,1,0:T(8,128)(2,1)S(1)}, bf16[8,128,2048]{2,1,0:T(8,128)(2,1)}, u32[]{:S(2)}) copy-start(bf16[8,128,2048]{2,1,0:T(8,128)(2,1)} %param.17) | copy-start | bytes 12582916
  102.1 30.7 %copy-start.5 = (bf16[128,2048]{1,0:T(8,128)(2,1)S(1)}, bf16[128,2048]{1,0:T(8,128)(2,1)}, u32[]{:S(2)}) copy-start(bf16[128,2048]{1,0:T(8,128)(2,1)} %param.12) | copy-start | bytes 1572868
  102.2 34.0 %copy-start.9 = (f32[128,2]{0,1:T(2,128)S(1)}, f32[128,2]{0,1:T(2,128)}, u32[]{:S(2)}) copy-start(f32[128,2]{0,1:T(2,128)} %param.21) | copy-start | bytes 3076
  102.2 34.0 %copy-start.10 = (s32[128,2]{0,1:T(2,128)S(1)}, s32[128,2]{0,1:T(2,128)}, u32[]{:S(2)}) copy-start(s32[128,2]{0,1:T(2,128)} %param.20) | copy-start | bytes 3076
  102.2 56.7 %all-gather.5.cloned.1.call-start = ((), (), s32[]{:S(2)}) async-start(), calls=%async_computation.6 | async-start | bytes 2621440 | tf_op jit(solution)/shard_map/all_gather | solution.py:247
  136.8 28.6 %all-to-all-start.1 = ((f32[4,1,128]{2,1,0:T(1,128)}), f32[4,1,128]{2,1,0:T(1,128)S(1)}, u32[]{:S(2)}, u32[]{:S(2)}) async-start(f32[4,1,128]{2,1,0:T(1,128)} %bitcast.2), calls=%async_computation.2 | async-start | bytes 4096 | tf_op jit(solution)/shard_map/all_to_all | solution.py:226
  139.9 61.2 %reduce-scatter.5.cloned.1.call-start = ((), (), s32[]{:S(2)}) async-start(), calls=%async_computation.7 | async-start | bytes 2621440 | tf_op jit(solution)/shard_map/reduce_scatter | solution.py:255
  169.6 31.6 %copy-start.6 = (bf16[128,2048]{1,0:T(8,128)(2,1)S(1)}, bf16[128,2048]{1,0:T(8,128)(2,1)}, u32[]{:S(2)}) copy-start(bf16[128,2048]{1,0:T(8,128)(2,1)} %reduce-scatter.3.cloned.1.call-done) | copy-start | bytes 1572868
Sparse Core Ops, SparseCore 0:
  10.7 25.2 all-gather.2
  102.3 30.4 reduce-scatter.2
  136.3 22.5 all-gather.4
  169.7 31.4 reduce-scatter.4

commit v2 on v1

v2 whole, which is shorter than its diff:
```python
from functools import partial

import jax
import jax.numpy as jnp
from jax import lax
from jax.experimental import pallas as pl
from jax.experimental.pallas import tpu as pltpu
from jax.sharding import PartitionSpec as P

EPSILON = 1e-06
HIGHEST = lax.Precision.HIGHEST
BF = jnp.bfloat16
F32 = jnp.float32


def rms_scale(values):
    return values * lax.rsqrt(jnp.mean(values * values, axis=-1, keepdims=True) + EPSILON)


def unit_length(values):
    return values * lax.rsqrt(jnp.sum(values * values, axis=-1, keepdims=True) + EPSILON)


def dot_nt(left, right):
    return lax.dot_general(
        left, right, (((1,), (1,)), ((), ())), preferred_element_type=F32
    )


def dot_tn(left, right):
    return lax.dot_general(
        left, right, (((0,), (0,)), ((), ())), preferred_element_type=F32
    )


def dot_nn(left, right):
    return jnp.dot(left, right, preferred_element_type=F32)


def pick_kernel(slot_ref, cache_ref, out_ref):
    out_ref[...] = cache_ref[...].astype(BF)


def pick_states(cache, slots):
    shape = cache.shape
    rows = slots.shape[0]
    block = (1,) + shape[1:]
    return pl.pallas_call(
        pick_kernel,
        grid_spec=pltpu.PrefetchScalarGridSpec(
            num_scalar_prefetch=1,
            grid=(rows,),
            in_specs=[pl.BlockSpec(block, lambda i, slot: (slot[i], 0, 0, 0))],
            out_specs=pl.BlockSpec(block, lambda i, slot: (i, 0, 0, 0)),
        ),
        out_shape=jax.ShapeDtypeStruct((rows,) + shape[1:], BF),
        compiler_params=pltpu.CompilerParams(vmem_limit_bytes=32 << 20),
    )(slots, cache)


def solve_kernel(qk_ref, rate_ref, decay_ref, unit_ref, inverse_ref, mixing_ref, coef_ref):
    length = qk_ref.shape[0]
    wide = inverse_ref.shape[-1]
    group = wide // length
    key_heads = inverse_ref.shape[1]
    key_size = qk_ref.shape[1] // (2 * key_heads)
    rate = rate_ref[...]
    beta = jax.nn.sigmoid(rate)
    log_decay = -decay_ref[...] * jax.nn.softplus(rate)
    row = lax.broadcasted_iota(jnp.int32, (length, length), 0)
    col = lax.broadcasted_iota(jnp.int32, (length, length), 1)
    lower = (col <= row).astype(F32)
    summed = jnp.dot(lower, log_decay, precision=HIGHEST, preferred_element_type=F32)
    summed_rows = summed.T
    closing = summed[length - 1 : length, :]
    coef_ref[...] = jnp.concatenate(
        [
            beta,
            jnp.exp(summed),
            jnp.exp(closing - summed),
            jnp.broadcast_to(jnp.exp(closing), summed.shape),
        ],
        axis=1,
    )

    wrow = lax.broadcasted_iota(jnp.int32, (wide, wide), 0)
    wcol = lax.broadcasted_iota(jnp.int32, (wide, wide), 1)
    same = wrow // length == wcol // length
    inclusive = same & (wcol <= wrow)
    strict = same & (wcol < wrow)
    eye = (wrow == wcol).astype(F32)

    belows = []
    for kh in range(key_heads):
        base = kh * 2 * key_size
        heads = range(kh * group, (kh + 1) * group)
        query = (unit_length(qk_ref[:, base : base + key_size]) * key_size ** (-0.5)).astype(BF)
        keys = unit_length(qk_ref[:, base + key_size : base + 2 * key_size]).astype(BF)
        unit_ref[0, kh] = jnp.concatenate([query, keys], axis=0)
        both = jnp.concatenate([query] * group + [keys] * group, axis=0)
        products = dot_nt(both, both[wide:])
        sum_col = jnp.concatenate([summed[:, 2 * h : 2 * h + 1] for h in heads], axis=0)
        sum_row = jnp.concatenate([summed_rows[2 * h : 2 * h + 1, :] for h in heads], axis=1)
        beta_col = jnp.concatenate([beta[:, 2 * h + 1 : 2 * h + 2] for h in heads], axis=0)
        spread = sum_col - sum_row
        ratio = jnp.where(inclusive, jnp.exp(jnp.minimum(spread, 0.0)), 0.0)
        belows.append(jnp.where(strict, beta_col * ratio * products[wide:], 0.0))
        mixing_ref[0, kh] = (ratio * products[:wide]).astype(BF)

    span = 1
    inverses = []
    while span < length:
        corner = (wrow // (2 * span) == wcol // (2 * span)) & (
            (wrow // span) % 2 == 1
        ) & ((wcol // span) % 2 == 0)
        corners = [jnp.where(corner, below, 0.0) for below in belows]
        if span == 1:
            inverses = [eye - c for c in corners]
        else:
            rounded = [t.astype(BF) for t in inverses]
            first = [dot_nn(c.astype(BF), t) for c, t in zip(corners, rounded)]
            inverses = [
                t - dot_nn(r, f.astype(BF)) for t, r, f in zip(inverses, rounded, first)
            ]
        span *= 2
    for kh in range(key_heads):
        inverse_ref[0, kh] = inverses[kh].astype(BF)


def state_kernel(
    source_ref, vz_ref, unit_ref, inverse_ref, mixing_ref, coef_ref, state_ref, gated_ref, final_ref
):
    length = vz_ref.shape[0]
    value_heads, size, key_size = state_ref.shape[1:]
    key_heads = inverse_ref.shape[1]
    group = value_heads // key_heads
    pairs = coef_ref.shape[1] // 4
    coef = coef_ref[...]

    def column(kind, h, at=0):
        place = kind * pairs + 2 * h + at
        return coef[:, place : place + 1]

    def stack(parts):
        return jnp.concatenate(list(parts), axis=0)

    carrieds = []
    for kh in range(key_heads):
        states = state_ref[0, kh * group : (kh + 1) * group].reshape(group * size, key_size)
        carrieds.append(dot_nt(unit_ref[0, kh], states))
    updates = []
    for kh in range(key_heads):
        heads = range(kh * group, (kh + 1) * group)
        beta_col = stack(column(0, h, 1) for h in heads)
        grow_col = stack(column(1, h) for h in heads)
        values = stack(vz_ref[:, 2 * h * size : (2 * h + 1) * size] for h in heads).astype(F32)
        key_part = stack(
            carrieds[kh][length:, i * size : (i + 1) * size] for i in range(group)
        )
        right_side = beta_col * (values - grow_col * key_part)
        updates.append(dot_nn(inverse_ref[0, kh], right_side.astype(BF)))
    readouts = []
    addeds = []
    for kh in range(key_heads):
        heads = range(kh * group, (kh + 1) * group)
        grow_col = stack(column(1, h) for h in heads)
        query_part = stack(
            carrieds[kh][:length, i * size : (i + 1) * size] for i in range(group)
        )
        readouts.append(
            grow_col * query_part + dot_nn(mixing_ref[0, kh], updates[kh].astype(BF))
        )
        tailed = [
            updates[kh][i * length : (i + 1) * length] * column(2, kh * group + i)
            for i in range(group)
        ]
        addeds.append(
            dot_tn(jnp.concatenate(tailed, axis=1).astype(BF), unit_ref[0, kh][length:])
        )
    for kh in range(key_heads):
        scaled = rms_scale(readouts[kh])
        for i in range(group):
            h = kh * group + i
            gate = vz_ref[:, (2 * h + 1) * size : (2 * h + 2) * size].astype(F32)
            gated_ref[:, h * size : (h + 1) * size] = (
                scaled[i * length : (i + 1) * length] * jax.nn.silu(gate)
            ).astype(BF)
            final_ref[0, h] = (
                column(3, h)[:1] * state_ref[0, h].astype(F32)
                + addeds[kh][i * size : (i + 1) * size]
            )


def solve_chunks(trajs, key_heads, value_heads, qk, rate, decay_pairs):
    length = qk.shape[0] // trajs
    wide = length * (value_heads // key_heads)
    key_size = qk.shape[1] // (2 * key_heads)
    rows = lambda width: pl.BlockSpec((length, width), lambda i: (i, 0))
    heads = lambda a, b: pl.BlockSpec((1, key_heads, a, b), lambda i: (i, 0, 0, 0))
    return pl.pallas_call(
        solve_kernel,
        grid=(trajs,),
        in_specs=[
            rows(qk.shape[1]),
            rows(rate.shape[1]),
            pl.BlockSpec((1, rate.shape[1]), lambda i: (0, 0)),
        ],
        out_specs=[
            heads(2 * length, key_size),
            heads(wide, wide),
            heads(wide, wide),
            rows(4 * rate.shape[1]),
        ],
        out_shape=[
            jax.ShapeDtypeStruct((trajs, key_heads, 2 * length, key_size), BF),
            jax.ShapeDtypeStruct((trajs, key_heads, wide, wide), BF),
            jax.ShapeDtypeStruct((trajs, key_heads, wide, wide), BF),
            jax.ShapeDtypeStruct((qk.shape[0], 4 * rate.shape[1]), F32),
        ],
        compiler_params=pltpu.CompilerParams(vmem_limit_bytes=32 << 20),
        cost_estimate=pl.CostEstimate(
            flops=trajs * key_heads * 26 * wide**3, bytes_accessed=6 << 20, transcendentals=0
        ),
    )(qk, rate, decay_pairs)


def apply_states(source, vz, unit, inverse, mixing, coef, states):
    trajs = source.shape[0]
    length = vz.shape[0] // trajs
    heads, size, key_size = states.shape[1:]
    rows = lambda width: pl.BlockSpec((length, width), lambda i, s: (i, 0))
    whole = lambda array: pl.BlockSpec((1,) + array.shape[1:], lambda i, s: (i, 0, 0, 0))
    return pl.pallas_call(
        state_kernel,
        grid_spec=pltpu.PrefetchScalarGridSpec(
            num_scalar_prefetch=1,
            grid=(trajs,),
            in_specs=[
                rows(vz.shape[1]),
                whole(unit),
                whole(inverse),
                whole(mixing),
                rows(coef.shape[1]),
                pl.BlockSpec((1, heads, size, key_size), lambda i, s: (s[i], 0, 0, 0)),
            ],
            out_specs=[
                rows(heads * size),
                pl.BlockSpec((1, heads, size, key_size), lambda i, s: (i, 0, 0, 0)),
            ],
        ),
        out_shape=[
            jax.ShapeDtypeStruct((vz.shape[0], heads * size), BF),
            jax.ShapeDtypeStruct((trajs, heads, size, key_size), F32),
        ],
        compiler_params=pltpu.CompilerParams(vmem_limit_bytes=32 << 20),
        cost_estimate=pl.CostEstimate(
            flops=trajs * heads * 8 * length * size * size, bytes_accessed=10 << 20, transcendentals=0
        ),
    )(source, vz, unit, inverse, mixing, coef, states)


def chunk_rows(rows):
    return max(16, rows // 4)


def enter(me, chips):
    core = me % 2
    barrier = pltpu.get_barrier_semaphore()
    pl.semaphore_signal(barrier, inc=1, device_id={"exp": me + 1 - 2 * core})
    for j in range(1, chips):
        mate = lax.rem(me // 2 + j, chips) * 2 + core
        pl.semaphore_signal(barrier, inc=1, device_id={"exp": mate})
    pl.semaphore_wait(barrier, chips)


def summed_chunks(me, chips, part_ref, near_ref, out_ref, far_ref, sems, finish):
    near_send, near_recv, far_send, far_recv = sems
    core, chip = me % 2, me // 2
    sibling = me + 1 - 2 * core
    rows = near_ref.shape[1]
    step = chunk_rows(rows)
    count = rows // step
    order = [(j, k) for j in list(range(1, chips)) + [0] for k in range(count)]

    def block(j, which, k):
        start = (lax.rem(chip + j, chips) * 2 + which) * rows + k * step
        return pl.ds(pl.multiple_of(start, step), step)

    near, far = {}, {}
    for j, k in order:
        near[j, k] = pltpu.make_async_remote_copy(
            src_ref=part_ref.at[block(j, 1 - core, k)],
            dst_ref=near_ref.at[j, pl.ds(k * step, step)],
            send_sem=near_send.at[j * count + k],
            recv_sem=near_recv.at[j * count + k],
            device_id={"exp": sibling},
        )
        near[j, k].start()
    for j, k in order:
        if j == 0:
            continue
        here = pl.ds(k * step, step)
        near[j, k].wait_recv()
        out_ref[j, here] = (
            part_ref[block(j, core, k)].astype(F32) + near_ref[j, here].astype(F32)
        ).astype(BF)
        far[j, k] = pltpu.make_async_remote_copy(
            src_ref=out_ref.at[j, here],
            dst_ref=far_ref.at[j, here],
            send_sem=far_send.at[j * count + k],
            recv_sem=far_recv.at[j * count + k],
            device_id={"exp": lax.rem(chip + j, chips) * 2 + core},
        )
        far[j, k].start()
    for k in range(count):
        here = pl.ds(k * step, step)
        near[0, k].wait_recv()
        total = part_ref[block(0, core, k)].astype(F32) + near_ref[0, here].astype(F32)
        for j in range(1, chips):
            far[j, k].wait_recv()
            total = total + far_ref[j, here].astype(F32)
        finish(k, here, total)
    return list(near.values()) + list(far.values())


def spread_kernel(
    chips, part_ref, tokens_ref, every_ref, hidden_ref, near_ref, out_ref, far_ref,
    near_send, near_recv, far_send, far_recv, share_send, share_recv, cross_send, cross_recv,
):
    me = lax.axis_index("exp")
    core, chip = me % 2, me // 2
    sibling = me + 1 - 2 * core
    rows = tokens_ref.shape[0]
    step = chunk_rows(rows)
    count = rows // step
    enter(me, chips)
    share, cross = {}, {}

    def place(owner, k):
        return pl.ds(pl.multiple_of(owner * rows + k * step, step), step)

    def send(where, j, k, device, send_sem, recv_sem):
        copy = pltpu.make_async_remote_copy(
            src_ref=every_ref.at[where],
            dst_ref=every_ref.at[where],
            send_sem=send_sem.at[j * count + k],
            recv_sem=recv_sem.at[j * count + k],
            device_id={"exp": device},
        )
        copy.start()
        return copy

    def finish(k, here, total):
        hidden = tokens_ref[here].astype(F32) + total
        hidden_ref[here] = hidden
        mine = place(me, k)
        every_ref[mine] = rms_scale(hidden).astype(BF)
        for j in range(1, chips):
            mate = lax.rem(chip + j, chips) * 2 + core
            cross[j, k] = send(mine, j, k, mate, cross_send, cross_recv)
        share[0, k] = send(mine, 0, k, sibling, share_send, share_recv)

    sems = (near_send, near_recv, far_send, far_recv)
    sent = summed_chunks(me, chips, part_ref, near_ref, out_ref, far_ref, sems, finish)
    for k in range(count):
        for j in range(1, chips):
            cross[j, k].wait_recv()
            owner = lax.rem(chip + chips - j, chips) * 2 + core
            share[j, k] = send(place(owner, k), j, k, sibling, share_send, share_recv)
    for copy in share.values():
        copy.wait_recv()
    for copy in sent + list(share.values()) + list(cross.values()):
        copy.wait_send()


def final_kernel(
    chips, part_ref, hidden_ref, result_ref, near_ref, out_ref, far_ref,
    near_send, near_recv, far_send, far_recv,
):
    me = lax.axis_index("exp")
    enter(me, chips)

    def finish(k, here, total):
        result_ref[here] = (hidden_ref[here] + total).astype(BF)

    sems = (near_send, near_recv, far_send, far_recv)
    sent = summed_chunks(me, chips, part_ref, near_ref, out_ref, far_ref, sems, finish)
    for copy in sent:
        copy.wait_send()


def remote_call(kernel, chips, collective_id, groups, out_shape, part, own):
    rows, model = own.shape
    copies = chips * (rows // chunk_rows(rows))
    vmem = pl.BlockSpec(memory_space=pltpu.VMEM)
    return pl.pallas_call(
        partial(kernel, chips),
        in_specs=[vmem, vmem],
        out_specs=jax.tree.map(lambda _: vmem, out_shape),
        out_shape=out_shape,
        scratch_shapes=[pltpu.VMEM((chips, rows, model), BF)] * 3
        + [pltpu.SemaphoreType.DMA((copies,))] * (2 * groups),
        compiler_params=pltpu.CompilerParams(
            collective_id=collective_id, has_side_effects=True, vmem_limit_bytes=48 << 20
        ),
    )(part, own)


def local(
    tokens,
    attend_weight,
    value_weight,
    rate_weight,
    decay_rate,
    output_weight,
    state_cache,
    resume_from,
    expert_index,
    route_weight,
    expert_inner,
    expert_outer,
):
    model = tokens.shape[1]
    value_heads = value_weight.shape[1]
    residual = tokens.astype(F32)
    normed = rms_scale(residual).astype(BF)
    piece = lax.all_gather(normed, "exp", axis=0, tiled=True)

    trajs = state_cache.shape[0]
    replicas = lax.axis_size("rep")
    myself = lax.axis_index("rep")
    my_rows = lax.dynamic_slice_in_dim(resume_from, myself * trajs, trajs)
    listing = resume_from.reshape(replicas, trajs)
    from_me = listing // trajs == myself
    slot_pick = jnp.sum(jnp.where(from_me, listing % trajs, 0), axis=1)
    outgoing = pick_states(state_cache, slot_pick)
    incoming = lax.all_to_all(outgoing, "rep", split_axis=0, concat_axis=0, tiled=True)

    local_experts = expert_inner.shape[0]
    total_experts = lax.axis_size("exp") * local_experts
    numbers = jnp.arange(total_experts, dtype=jnp.int32)
    share = jnp.sum(
        jnp.where(expert_index[None] == numbers[:, None, None], route_weight[None], 0.0), axis=2
    )
    shares = lax.all_to_all(
        share.reshape(lax.axis_size("exp"), local_experts, -1),
        "exp", split_axis=0, concat_axis=0, tiled=True,
    )
    shares = jnp.moveaxis(shares, 1, 0).reshape(local_experts, -1)

    qk = jnp.dot(piece, attend_weight.reshape(model, -1), preferred_element_type=F32)
    vz = jnp.dot(piece, value_weight.reshape(model, -1), preferred_element_type=F32).astype(BF)
    rate = jnp.dot(piece, rate_weight.reshape(model, -1), preferred_element_type=F32)
    decay_pairs = jnp.repeat(decay_rate, 2)[None, :]
    solved = solve_chunks(trajs, attend_weight.shape[1], value_heads, qk, rate, decay_pairs)
    gated, final_state = apply_states(my_rows // trajs, vz, *solved, incoming)

    output_flat = output_weight.reshape(-1, model)
    partial_rows = jnp.dot(gated, output_flat, preferred_element_type=F32).astype(BF)
    chips = lax.axis_size("exp") // 2
    everyone, hidden = remote_call(
        spread_kernel,
        chips,
        0,
        4,
        [
            jax.ShapeDtypeStruct(partial_rows.shape, BF),
            jax.ShapeDtypeStruct(tokens.shape, F32),
        ],
        partial_rows,
        tokens,
    )
    inner = expert_outer.shape[1]
    weighted = 0.0
    for e in range(local_experts):
        both_parts = jnp.dot(everyone, expert_inner[e], preferred_element_type=F32)
        activated = (jax.nn.silu(both_parts[:, :inner]) * both_parts[:, inner:]).astype(BF)
        produced = jnp.dot(activated, expert_outer[e], preferred_element_type=F32)
        weighted = weighted + shares[e][:, None] * produced
    layer_output = remote_call(
        final_kernel,
        chips,
        1,
        2,
        jax.ShapeDtypeStruct(tokens.shape, BF),
        weighted.astype(BF),
        hidden,
    )
    return (layer_output, final_state)


def solution(mesh):
    in_specs = (
        P(("rep", "exp"), None),
        P(None, "exp", None),
        P(None, "exp", None),
        P(None, "exp", None),
        P("exp"),
        P("exp", None, None),
        P("rep", "exp", None, None),
        P(),
        P(("rep", "exp"), None),
        P(("rep", "exp"), None),
        P("exp", None, None),
        P("exp", None, None),
    )
    out_specs = (P(("rep", "exp"), None), P("rep", "exp", None, None))
    return jax.shard_map(local, mesh=mesh, in_specs=in_specs, out_specs=out_specs, check_vma=False)
```

time: 210 us -> 150 us (0.71)
  waiting for transfers between devices: 101 us -> 2.77 us
  Pallas kernels: 25.3 us -> 70.7 us
  matrix products: 29.3 us -> 22.2 us
  other arithmetic: 9.56 us -> 4.16 us
  local copies, waits for them, and re-layouts: 20.6 us -> 24.2 us
    reduce_scatter x2 -> x0, waiting for transfers between devices: 62.2 us -> none  [the longest x1 31.6 us: local(): lax.psum_scatter(weighted.astype(BF), 'exp', scatter_dimension=0, tiled=T...]
    pallas_call x1 -> x4, Pallas kernels: 24.4 us -> 69.8 us  [the longest x2 44.3 us: remote_call(): pl.pallas_call(partial(kernel, chips), in_specs=[vmem, vmem], out_specs=j...]
    all_gather x1 -> x0, waiting for transfers between devices: 18.9 us -> none  [local(): everyone = lax.all_gather(hidden_normed, 'exp', axis=0, tiled=True)]
    all_to_all x1, waiting for transfers between devices: 19.5 us -> 2.75 us  [local(): lax.all_to_all(outgoing, 'rep', split_axis=0, concat_axis=0, tiled=True)]
    convert_element_type x2 -> x0, other arithmetic: 4.09 us -> none  [the longest x1 2.08 us: local(): layer_output = (hidden + expert_sum).astype(BF)]
    unnamed x36 -> x43, local copies, waits for them, and re-layouts: 20.3 us -> 23.9 us
    dot_general x1, matrix products: 6.49 us -> 3.66 us  [local(): both_parts = jnp.dot(everyone, expert_inner[e], preferred_element_type=F32)]
  transfers between devices with their start and end apart: 6 -> 3, of which waited for: 4 -> 1; matrix products, arithmetic and copies ran while one was open for 17% -> 23% of each run, Pallas kernels for 0% -> 37%
where the time goes in v2:
time: 150 us; the launch traced here: 149 us
  Pallas kernels  70.7 us (47%)
  local copies, waits for them, and re-layouts  24.2 us (16%)
  matrix products  22.2 us (15%)
  between operations  14.2 us (9%)
  starting transfers between devices  10.7 us (7%)
  other arithmetic  4.16 us (3%)
  waiting for transfers between devices  2.77 us (2%)
    pallas_call x2, Pallas kernels, remote_call(): pl.pallas_call(partial(kernel, chips), in_specs=[vmem, vmem], out_specs=j...  44.3 us
    unnamed x43, local copies, waits for them, and re-layouts  23.9 us
    pallas_call x1, Pallas kernels, solve_chunks(): pl.pallas_call(solve_kernel, grid=(trajs,), in_specs=[rows(qk.shape[1]),...  15.7 us
    pallas_call x1, Pallas kernels, apply_states(): pl.pallas_call(state_kernel, grid_spec=pltpu.PrefetchScalarGridSpec(num_s...  9.77 us
    all_to_all x1, starting transfers between devices, local(): lax.all_to_all(outgoing, 'rep', split_axis=0, concat_axis=0, tiled=True)  7.28 us
    dot_general x1, matrix products, local(): jnp.dot(piece, value_weight.reshape(model, -1), preferred_element_type=F32)  5.67 us
    dot_general x1, matrix products, local(): jnp.dot(piece, attend_weight.reshape(model, -1), preferred_element_type=F32)  5.3 us
    dot_general x1, matrix products, local(): both_parts = jnp.dot(everyone, expert_inner[e], preferred_element_type=F32)  3.66 us
  transfers between devices with their start and end apart: 3, of which 1 were waited for; matrix products, arithmetic and copies ran while one was open for 23% of the time, Pallas kernels for 37%

profile of v2, /device:TPU:0, one launch (start us, length us, event | category | flops | bytes accessed | tf_op | source)
XLA Modules:
  0.0 148.9 jit_solution(13917557681478995072)
XLA Ops:
  7.2 1.4 fusion.3
  8.6 2.0 %fusion.4 = bf16[128,2048]{1,0:T(8,128)(2,1)} fusion(bf16[128,2048]{1,0:T(8,128)(2,1)} %tokens_ref.1, f32[128]{0:T(128)S(1)} %add_rsqrt_fusion), kind=kLoop, calls=%fused_computation.9 | loop fusion | flops 786432 | bytes 1049088 | tf_op jit(solution)/shard_map/convert_element_type | solution.py:426
  10.6 0.1 reshape.37
  10.7 0.1 fusion.10.slot_ref
  10.9 2.2 %copy-done.3 = f32[8,8,128,128]{3,2,1,0:T(8,128)S(1)} copy-done((f32[8,8,128,128]{3,2,1,0:T(8,128)S(1)}, f32[8,8,128,128]{3,2,1,0:T(8,128)}, u32[]{:S(2)}) %copy-start.3) | copy-done | bytes 4194328
  13.0 0.9 shard_map.132
  13.9 1.3 copy-done.1
  15.3 7.3 %all-to-all-start.1 = ((bf16[8,8,128,128]{3,2,1,0:T(8,128)(2,1)}), bf16[8,8,128,128]{3,2,1,0:T(8,128)(2,1)}, u32[]{:S(2)}, u32[]{:S(2)}) async-start(bf16[8,8,128,128]{3,2,1,0:T(8,128)(2,1)} %copy-done.1), calls=%async_computation.1 | async-start | bytes 4194304 | tf_op jit(solution)/shard_map/all_to_all | solution.py:437
  22.5 10.5 %copy.26 = bf16[256,8,8,256]{3,1,2,0:T(8,128)(2,1)} copy(bf16[256,8,8,256]{3,2,1,0:T(8,128)(2,1)} %bitcast.26) | data formatting | bytes 16777216
  33.1 3.1 %copy.27 = bf16[256,8,4,256]{3,1,2,0:T(8,128)(2,1)} copy(bf16[256,8,4,256]{3,2,1,0:T(4,128)(2,1)S(1)} %bitcast.30) | data formatting | bytes 8388608
  36.2 0.1 broadcast_in_dim.23
  36.2 0.1 broadcast_in_dim_reshape.3.decay_ref
  36.3 0.1 and_select_fusion.source_ref
  36.4 0.6 select_reduce_fusion
  37.0 2.4 %fusion.15.rate_ref = f32[512,16]{1,0:T(8,128)S(1)} fusion(bf16[512,2048]{1,0:T(8,128)(2,1)} %all-gather.2.cloned.1.call-done, bf16[2048,16]{0,1:T(8,128)(2,1)S(1)} %reshape.36), kind=kOutput, calls=%fused_computation.33 | convolution fusion | flops 33554432 | bytes 2195456 | tf_op jit(solution)/shard_map/dot_general | solution.py:453
  39.4 5.3 %fusion.14.qk_ref = f32[512,1024]{1,0:T(8,128)S(1)} fusion(bf16[512,2048]{1,0:T(8,128)(2,1)} %all-gather.2.cloned.1.call-done, bf16[2048,1024]{1,0:T(8,128)(2,1)} %bitcast.31), kind=kOutput, calls=%fused_computation.32 | convolution fusion | flops 2147483648 | bytes 8388608 | tf_op jit(solution)/shard_map/dot_general | solution.py:451
  44.8 15.7 %shard_map.131 = (bf16[8,4,128,128]{3,2,1,0:T(8,128)(2,1)S(1)}, bf16[8,4,128,128]{3,2,1,0:T(8,128)(2,1)S(1)}, bf16[8,4,128,128]{3,2,1,0:T(8,128)(2,1)S(1)}, f32[512,64]{1,0:T(8,128)S(1)}) custom-call(f32[512,1024]{1,0:T(8,128)S(1)} %fusion.14.qk_ref, f32[512,16]{1,0:T(8,128)S(1)} %fusion.15.rate_ref, f32[1,16]{1,0:T(1,128)S(1)} %broadcast_in_dim_reshape.3.decay_ref), custom_call_target="tpu_custom_call" | custom-call | flops 1744830464 | bytes 6291456 | tf_op jit(solution)/shard_map/pallas_call | solution.py:200
  60.5 1.0 copy-done.5
  61.5 1.0 copy-done.7
  62.5 5.7 %convolution_convert_fusion.1.vz_ref = bf16[512,2048]{1,0:T(8,128)(2,1)} fusion(bf16[512,2048]{1,0:T(8,128)(2,1)S(1)} %copy-done.17, bf16[2048,2048]{1,0:T(8,128)(2,1)S(1)} %bitcast.29), kind=kOutput, calls=%fused_computation.4 | convolution fusion | flops 4296015872 | bytes 12582912 | tf_op jit(solution)/shard_map/dot_general | solution.py:452
  68.1 2.8 %all-to-all-done.1.state_ref = bf16[8,8,128,128]{3,2,1,0:T(8,128)(2,1)} async-done(((bf16[8,8,128,128]{3,2,1,0:T(8,128)(2,1)}), bf16[8,8,128,128]{3,2,1,0:T(8,128)(2,1)}, u32[]{:S(2)}, u32[]{:S(2)}) %all-to-all-start.1) | async-done | bytes 2097184 | tf_op jit(solution)/shard_map/all_to_all | solution.py:437
  70.9 3.4 %all-to-all-start = ((f32[4,1,128]{2,1,0:T(1,128)}), f32[4,1,128]{2,1,0:T(1,128)S(1)}, u32[]{:S(2)}, u32[]{:S(2)}) async-start(f32[4,1,128]{2,1,0:T(1,128)} %bitcast.1), calls=%async_computation | async-start | bytes 4096 | tf_op jit(solution)/shard_map/all_to_all | solution.py:445
  74.3 1.6 %copy-done.4 = bf16[512,2048]{1,0:T(8,128)(2,1)S(1)} copy-done((bf16[512,2048]{1,0:T(8,128)(2,1)S(1)}, bf16[512,2048]{1,0:T(8,128)(2,1)}, u32[]{:S(2)}) %copy-start.4) | copy-done | bytes 2097176
  75.9 1.2 copy-done.6
  77.1 1.2 copy-done.8
  78.3 9.8 %shard_map.133 = (bf16[512,1024]{1,0:T(8,128)(2,1)S(1)}, f32[8,8,128,128]{3,2,1,0:T(8,128)}) custom-call(s32[8]{0:T(128)S(1)} %and_select_fusion.source_ref, bf16[512,2048]{1,0:T(8,128)(2,1)S(1)} %copy-done.4, bf16[8,4,128,128]{3,2,1,0:T(8,128)(2,1)S(1)} %get-tuple-element.10.unit_ref, bf16[8,4,128,128]{3,2,1,0:T(8,128)(2,1)S(1)} %copy-done.6, ...), custom_call_target="tpu_custom_call" | custom-call | flops 536870912 | bytes 10485760 | tf_op jit(solution)/shard_map/pallas_call | solution.py:233
  88.1 2.3 %convolution_convert_fusion.part_ref = bf16[512,2048]{1,0:T(8,128)(2,1)S(1)} fusion(bf16[512,1024]{1,0:T(8,128)(2,1)S(1)} %get-tuple-element.14, bf16[1024,2048]{1,0:T(8,128)(2,1)S(1)} %bitcast.33), kind=kOutput, calls=%fused_computation.3 | convolution fusion | flops 2148532224 | bytes 7340032 | tf_op jit(solution)/shard_map/dot_general | solution.py:459
  90.4 28.3 %shard_map.134 = (bf16[512,2048]{1,0:T(8,128)(2,1)S(1)}, f32[128,2048]{1,0:T(8,128)S(1)}) custom-call(bf16[512,2048]{1,0:T(8,128)(2,1)S(1)} %convolution_convert_fusion.part_ref, bf16[128,2048]{1,0:T(8,128)(2,1)S(1)} %copy-done.2), custom_call_target="tpu_custom_call" | custom-call | tf_op jit(solution)/shard_map/pallas_call | solution.py:396
  118.8 3.7 %fusion = f32[512,1024]{1,0:T(8,128)} fusion(bf16[512,2048]{1,0:T(8,128)(2,1)S(1)} %get-tuple-element.15, bf16[1,2048,1024]{2,1,0:T(8,128)(2,1)S(1)} %copy-done.16), kind=kOutput, calls=%fused_computation | convolution fusion | flops 2147483648 | bytes 8388608 | tf_op jit(solution)/shard_map/dot_general | solution.py:476
  122.4 2.8 %multiply_convert_fusion.part_ref = bf16[512,2048]{1,0:T(8,128)(2,1)S(1)} fusion(bf16[1,512,2048]{2,1,0:T(8,128)(2,1)S(1)} %copy-done, f32[512]{0:T(512)S(1)} %bitcast.32, f32[512,1024]{1,0:T(8,128)} %fusion), kind=kOutput, calls=%fused_computation.2 | convolution fusion | flops 1077411840 | bytes 6293504 | tf_op jit(solution)/shard_map/dot_general | solution.py:478
  125.3 16.0 %shard_map.135 = bf16[128,2048]{1,0:T(8,128)(2,1)S(1)} custom-call(bf16[512,2048]{1,0:T(8,128)(2,1)S(1)} %multiply_convert_fusion.part_ref, f32[128,2048]{1,0:T(8,128)S(1)} %get-tuple-element.16.hidden_ref), custom_call_target="tpu_custom_call" | custom-call | tf_op jit(solution)/shard_map/pallas_call | solution.py:396
  141.3 0.8 copy.29
  (40 shorter events, 0.2 us)
Async XLA Ops:
  7.2 115.3 %copy-start = (bf16[1,512,2048]{2,1,0:T(8,128)(2,1)S(1)}, bf16[1,512,2048]{2,1,0:T(8,128)(2,1)}, u32[]{:S(2)}) copy-start(bf16[1,512,2048]{2,1,0:T(8,128)(2,1)} %param.23) | copy-start | bytes 6291460
  7.2 3.5 %copy-start.14 = (s32[64]{0:T(128)S(1)}, s32[64]{0:T(128)}, u32[]{:S(2)}) copy-start(s32[64]{0:T(128)} %param.19) | copy-start | bytes 772
  7.2 29.8 %all-gather.2.cloned.1.call-start = ((), (), s32[]{:S(2)}) async-start(), calls=%async_computation.2 | async-start | bytes 2621440 | tf_op jit(solution)/shard_map/all_gather | solution.py:427
  10.8 2.2 %copy-start.3 = (f32[8,8,128,128]{3,2,1,0:T(8,128)S(1)}, f32[8,8,128,128]{3,2,1,0:T(8,128)}, u32[]{:S(2)}) copy-start(f32[8,8,128,128]{3,2,1,0:T(8,128)} %cache_ref.1) | copy-start | bytes 12582916
  13.9 1.3 copy-start.1
  15.3 55.6 %all-to-all-start.1 = ((bf16[8,8,128,128]{3,2,1,0:T(8,128)(2,1)}), bf16[8,8,128,128]{3,2,1,0:T(8,128)(2,1)}, u32[]{:S(2)}, u32[]{:S(2)}) async-start(bf16[8,8,128,128]{3,2,1,0:T(8,128)(2,1)} %copy-done.1), calls=%async_computation.1 | async-start | bytes 4194304 | tf_op jit(solution)/shard_map/all_to_all | solution.py:437
  22.5 10.5 %copy-start.9 = (bf16[2048,4,256]{2,1,0:T(4,128)(2,1)S(1)}, bf16[2048,4,256]{2,1,0:T(4,128)(2,1)}, u32[]{:S(2)}) copy-start(bf16[2048,4,256]{2,1,0:T(4,128)(2,1)} %param.13) | copy-start | bytes 12582916
  33.0 3.1 %copy-start.10 = (bf16[2048,8,2]{0,2,1:T(2,128)(2,1)S(1)}, bf16[2048,8,2]{0,2,1:T(2,128)(2,1)}, u32[]{:S(2)}) copy-start(bf16[2048,8,2]{0,2,1:T(2,128)(2,1)} %param.15) | copy-start | bytes 196612
  33.0 3.1 %copy-start.13 = (f32[8]{0:T(128)S(1)}, f32[8]{0:T(128)}, u32[]{:S(2)}) copy-start(f32[8]{0:T(128)} %param.16) | copy-start | bytes 100
  33.0 3.4 %copy-start.11 = (f32[128,2]{0,1:T(2,128)S(1)}, f32[128,2]{0,1:T(2,128)}, u32[]{:S(2)}) copy-start(f32[128,2]{0,1:T(2,128)} %param.21) | copy-start | bytes 3076
  33.1 3.3 %copy-start.12 = (s32[128,2]{0,1:T(2,128)S(1)}, s32[128,2]{0,1:T(2,128)}, u32[]{:S(2)}) copy-start(s32[128,2]{0,1:T(2,128)} %param.20) | copy-start | bytes 3076
  37.0 25.5 %slice-start = ((s8[8388608]{0:T(1024)(128)(4,1)}), s8[4194304]{0:T(1024)(128)(4,1)S(1)}, s32[]{:S(2)}) async-start(s8[8388608]{0:T(1024)(128)(4,1)} %bitcast.27), calls=%async_computation.3 | async-start | bytes 8388608
  39.4 23.0 %slice-start.1 = ((s8[8388608]{0:T(1024)(128)(4,1)}), s8[4194304]{0:T(1024)(128)(4,1)S(1)}, s32[]{:S(2)}) async-start(s8[8388608]{0:T(1024)(128)(4,1)} %bitcast.27), calls=%async_computation.4 | async-start | bytes 8388608
  44.7 17.7 %copy-start.17 = (bf16[512,2048]{1,0:T(8,128)(2,1)S(1)}, bf16[512,2048]{1,0:T(8,128)(2,1)}, u32[]{:S(2)}) copy-start(bf16[512,2048]{1,0:T(8,128)(2,1)} %all-gather.2.cloned.1.call-done) | copy-start | bytes 6291460
  60.5 1.0 copy-start.5
  61.5 1.0 copy-start.7
  70.9 51.6 %all-to-all-start = ((f32[4,1,128]{2,1,0:T(1,128)}), f32[4,1,128]{2,1,0:T(1,128)S(1)}, u32[]{:S(2)}, u32[]{:S(2)}) async-start(f32[4,1,128]{2,1,0:T(1,128)} %bitcast.1), calls=%async_computation | async-start | bytes 4096 | tf_op jit(solution)/shard_map/all_to_all | solution.py:445
  74.3 1.6 %copy-start.4 = (bf16[512,2048]{1,0:T(8,128)(2,1)S(1)}, bf16[512,2048]{1,0:T(8,128)(2,1)}, u32[]{:S(2)}) copy-start(bf16[512,2048]{1,0:T(8,128)(2,1)} %convolution_convert_fusion.1.vz_ref) | copy-start | bytes 6291460
  75.9 1.2 copy-start.6
  77.1 1.2 copy-start.8
  78.3 9.8 %copy-start.15 = (bf16[8,128,2048]{2,1,0:T(8,128)(2,1)S(1)}, bf16[8,128,2048]{2,1,0:T(8,128)(2,1)}, u32[]{:S(2)}) copy-start(bf16[8,128,2048]{2,1,0:T(8,128)(2,1)} %param.17) | copy-start | bytes 12582916
  88.1 2.4 %copy-start.2 = (bf16[128,2048]{1,0:T(8,128)(2,1)S(1)}, bf16[128,2048]{1,0:T(8,128)(2,1)}, u32[]{:S(2)}) copy-start(bf16[128,2048]{1,0:T(8,128)(2,1)} %tokens_ref.1) | copy-start | bytes 1572868
  88.1 30.7 %copy-start.16 = (bf16[1,2048,1024]{2,1,0:T(8,128)(2,1)S(1)}, bf16[1,2048,1024]{2,1,0:T(8,128)(2,1)}, u32[]{:S(2)}) copy-start(bf16[1,2048,1024]{2,1,0:T(8,128)(2,1)} %param.22) | copy-start | bytes 12582916
Sparse Core Ops, SparseCore 0:
  10.7 25.2 all-gather.1

commit v3 on v2

--- a/solution.py
+++ b/solution.py
@@ -442,9 +442,8 @@
     share = jnp.sum(
         jnp.where(expert_index[None] == numbers[:, None, None], route_weight[None], 0.0), axis=2
     )
-    shares = lax.all_to_all(
-        share.reshape(lax.axis_size("exp"), local_experts, -1),
-        "exp", split_axis=0, concat_axis=0, tiled=True,
+    shares = lax.dynamic_slice_in_dim(
+        lax.all_gather(share, "exp"), lax.axis_index("exp") * local_experts, local_experts, axis=1
     )
     shares = jnp.moveaxis(shares, 1, 0).reshape(local_experts, -1)
 

time: 150 us -> 145 us (0.967)
  blocking collectives: 0 us -> 5.17 us
  starting transfers between devices: 10.7 us -> 7.32 us
  matrix products: 22.2 us -> 19.3 us
  waiting for transfers between devices: 2.77 us -> 0.04 us
    all_gather x0 -> x1, blocking collectives: none -> 5.17 us  [local(): lax.all_gather(share, 'exp')]
    all_to_all x1 -> x0, starting transfers between devices: 3.37 us -> none  [local(): lax.all_to_all(share.reshape(lax.axis_size('exp'), local_experts, -1), 'e...]
    all_to_all x1, waiting for transfers between devices: 2.75 us -> 0.01 us  [local(): lax.all_to_all(outgoing, 'rep', split_axis=0, concat_axis=0, tiled=True)]
    dot_general x1, matrix products: 2.83 us -> 1.29 us  [local(): produced = jnp.dot(activated, expert_outer[e], preferred_element_type=F32)]
  transfers between devices with their start and end apart: 3 -> 2, of which waited for: 1 -> 0; matrix products, arithmetic and copies ran while one was open for 23% -> 19% of each run, Pallas kernels for 37% -> 12%
where the time goes in v3:
time: 145 us
  Pallas kernels  70.8 us (49%)
  local copies, waits for them, and re-layouts  24.2 us (17%)
  matrix products  19.3 us (13%)
  between operations  14.3 us (10%)
  starting transfers between devices  7.32 us (5%)
  blocking collectives  5.17 us (4%)
  other arithmetic  3.59 us (2%)
    pallas_call x2, Pallas kernels, remote_call(): pl.pallas_call(partial(kernel, chips), in_specs=[vmem, vmem], out_specs=j...  44.2 us
    unnamed x43, local copies, waits for them, and re-layouts  23.9 us
    pallas_call x1, Pallas kernels, solve_chunks(): pl.pallas_call(solve_kernel, grid=(trajs,), in_specs=[rows(qk.shape[1]),...  15.9 us
    pallas_call x1, Pallas kernels, apply_states(): pl.pallas_call(state_kernel, grid_spec=pltpu.PrefetchScalarGridSpec(num_s...  9.8 us
    all_to_all x1, starting transfers between devices, local(): lax.all_to_all(outgoing, 'rep', split_axis=0, concat_axis=0, tiled=True)  7.28 us
    dot_general x1, matrix products, local(): jnp.dot(piece, value_weight.reshape(model, -1), preferred_element_type=F32)  5.67 us
    dot_general x1, matrix products, local(): jnp.dot(piece, attend_weight.reshape(model, -1), preferred_element_type=F32)  5.3 us
    all_gather x1, blocking collectives, local(): lax.all_gather(share, 'exp')  5.17 us
  transfers between devices with their start and end apart: 2, of which 0 were waited for; matrix products, arithmetic and copies ran while one was open for 19% of the time, Pallas kernels for 12%

profile of v3, /device:TPU:0, one launch (start us, length us, event | category | flops | bytes accessed | tf_op | source)
XLA Modules:
  0.0 144.7 jit_solution(1123549374326220688)
XLA Ops:
  7.2 0.0 all-gather.4.cloned.1.call-start
  7.2 1.4 fusion.3
  8.6 2.0 %fusion.4 = bf16[128,2048]{1,0:T(8,128)(2,1)} fusion(bf16[128,2048]{1,0:T(8,128)(2,1)} %tokens_ref.1, f32[128]{0:T(128)S(1)} %add_rsqrt_fusion), kind=kLoop, calls=%fused_computation.9 | loop fusion | flops 786432 | bytes 1049088 | tf_op jit(solution)/shard_map/convert_element_type | solution.py:426
  10.6 0.1 reshape.33
  10.7 0.1 fusion.10.slot_ref
  10.9 2.2 %copy-done.3 = f32[8,8,128,128]{3,2,1,0:T(8,128)S(1)} copy-done((f32[8,8,128,128]{3,2,1,0:T(8,128)S(1)}, f32[8,8,128,128]{3,2,1,0:T(8,128)}, u32[]{:S(2)}) %copy-start.3) | copy-done | bytes 4194328
  13.0 0.9 shard_map.132
  13.9 1.3 copy-done.1
  15.3 7.3 %all-to-all-start = ((bf16[8,8,128,128]{3,2,1,0:T(8,128)(2,1)}), bf16[8,8,128,128]{3,2,1,0:T(8,128)(2,1)}, u32[]{:S(2)}, u32[]{:S(2)}) async-start(bf16[8,8,128,128]{3,2,1,0:T(8,128)(2,1)} %copy-done.1), calls=%async_computation | async-start | bytes 4194304 | tf_op jit(solution)/shard_map/all_to_all | solution.py:437
  22.6 10.5 %copy.25 = bf16[256,8,8,256]{3,1,2,0:T(8,128)(2,1)} copy(bf16[256,8,8,256]{3,2,1,0:T(8,128)(2,1)} %bitcast.24) | data formatting | bytes 16777216
  33.1 3.1 %copy.26 = bf16[256,8,4,256]{3,1,2,0:T(8,128)(2,1)} copy(bf16[256,8,4,256]{3,2,1,0:T(4,128)(2,1)S(1)} %bitcast.28) | data formatting | bytes 8388608
  36.2 0.1 broadcast_in_dim.23
  36.2 0.1 broadcast_in_dim_reshape.3.decay_ref
  36.3 5.2 %all-gather.1 = f32[4,4,128]{2,1,0:T(4,128)S(1)} all-gather(f32[1,4,128]{2,1,0:T(4,128)S(1)} %bitcast.30), channel_id=2, replica_groups=mesh['rep'=8,'exp'=4] {'exp'}, dimensions={0}, use_global_device_ids=true | all-gather | bytes 10240 | tf_op jit(solution)/shard_map/all_gather | solution.py:446
  41.5 0.1 and_select_fusion.source_ref
  41.6 0.0 all-gather.4.cloned.1.call-done
  41.6 2.4 %fusion.15.rate_ref = f32[512,16]{1,0:T(8,128)S(1)} fusion(bf16[512,2048]{1,0:T(8,128)(2,1)} %all-gather.4.cloned.1.call-done, bf16[2048,16]{0,1:T(8,128)(2,1)S(1)} %reshape.32), kind=kOutput, calls=%fused_computation.34 | convolution fusion | flops 33554432 | bytes 2195456 | tf_op jit(solution)/shard_map/dot_general | solution.py:452
  44.1 5.3 %fusion.14.qk_ref = f32[512,1024]{1,0:T(8,128)S(1)} fusion(bf16[512,2048]{1,0:T(8,128)(2,1)} %all-gather.4.cloned.1.call-done, bf16[2048,1024]{1,0:T(8,128)(2,1)} %bitcast.29), kind=kOutput, calls=%fused_computation.33 | convolution fusion | flops 2147483648 | bytes 8388608 | tf_op jit(solution)/shard_map/dot_general | solution.py:450
  49.4 15.9 %shard_map.131 = (bf16[8,4,128,128]{3,2,1,0:T(8,128)(2,1)S(1)}, bf16[8,4,128,128]{3,2,1,0:T(8,128)(2,1)S(1)}, bf16[8,4,128,128]{3,2,1,0:T(8,128)(2,1)S(1)}, f32[512,64]{1,0:T(8,128)S(1)}) custom-call(f32[512,1024]{1,0:T(8,128)S(1)} %fusion.14.qk_ref, f32[512,16]{1,0:T(8,128)S(1)} %fusion.15.rate_ref, f32[1,16]{1,0:T(1,128)S(1)} %broadcast_in_dim_reshape.3.decay_ref), custom_call_target="tpu_custom_call" | custom-call | flops 1744830464 | bytes 6291456 | tf_op jit(solution)/shard_map/pallas_call | solution.py:200
  65.3 1.0 copy-done.5
  66.3 1.0 copy-done.7
  67.3 5.7 %convolution_convert_fusion.1.vz_ref = bf16[512,2048]{1,0:T(8,128)(2,1)} fusion(bf16[512,2048]{1,0:T(8,128)(2,1)S(1)} %copy-done.17, bf16[2048,2048]{1,0:T(8,128)(2,1)S(1)} %bitcast.27), kind=kOutput, calls=%fused_computation.4 | convolution fusion | flops 4296015872 | bytes 12582912 | tf_op jit(solution)/shard_map/dot_general | solution.py:451
  73.0 1.6 %copy-done.4 = bf16[512,2048]{1,0:T(8,128)(2,1)S(1)} copy-done((bf16[512,2048]{1,0:T(8,128)(2,1)S(1)}, bf16[512,2048]{1,0:T(8,128)(2,1)}, u32[]{:S(2)}) %copy-start.4) | copy-done | bytes 2097176
  74.5 1.2 copy-done.6
  75.8 1.2 copy-done.8
  77.0 9.8 %shard_map.133 = (bf16[512,1024]{1,0:T(8,128)(2,1)S(1)}, f32[8,8,128,128]{3,2,1,0:T(8,128)}) custom-call(s32[8]{0:T(128)S(1)} %and_select_fusion.source_ref, bf16[512,2048]{1,0:T(8,128)(2,1)S(1)} %copy-done.4, bf16[8,4,128,128]{3,2,1,0:T(8,128)(2,1)S(1)} %get-tuple-element.10.unit_ref, bf16[8,4,128,128]{3,2,1,0:T(8,128)(2,1)S(1)} %copy-done.6, ...), custom_call_target="tpu_custom_call" | custom-call | flops 536870912 | bytes 10485760 | tf_op jit(solution)/shard_map/pallas_call | solution.py:233
  86.8 2.3 %convolution_convert_fusion.part_ref = bf16[512,2048]{1,0:T(8,128)(2,1)S(1)} fusion(bf16[512,1024]{1,0:T(8,128)(2,1)S(1)} %get-tuple-element.14, bf16[1024,2048]{1,0:T(8,128)(2,1)S(1)} %bitcast.32), kind=kOutput, calls=%fused_computation.3 | convolution fusion | flops 2148532224 | bytes 7340032 | tf_op jit(solution)/shard_map/dot_general | solution.py:458
  89.2 28.3 %shard_map.134 = (bf16[512,2048]{1,0:T(8,128)(2,1)S(1)}, f32[128,2048]{1,0:T(8,128)S(1)}) custom-call(bf16[512,2048]{1,0:T(8,128)(2,1)S(1)} %convolution_convert_fusion.part_ref, bf16[128,2048]{1,0:T(8,128)(2,1)S(1)} %copy-done.2), custom_call_target="tpu_custom_call" | custom-call | tf_op jit(solution)/shard_map/pallas_call | solution.py:396
  117.5 2.3 %fusion = f32[512,1024]{1,0:T(8,128)S(1)} fusion(bf16[512,2048]{1,0:T(8,128)(2,1)S(1)} %get-tuple-element.15, bf16[1,2048,1024]{2,1,0:T(8,128)(2,1)S(1)} %copy-done.16), kind=kOutput, calls=%fused_computation | convolution fusion | flops 2147483648 | bytes 8388608 | tf_op jit(solution)/shard_map/dot_general | solution.py:475
  119.8 1.3 multiply_convert_fusion.part_ref
  121.1 15.9 %shard_map.135 = bf16[128,2048]{1,0:T(8,128)(2,1)S(1)} custom-call(bf16[512,2048]{1,0:T(8,128)(2,1)S(1)} %multiply_convert_fusion.part_ref, f32[128,2048]{1,0:T(8,128)S(1)} %get-tuple-element.16.hidden_ref), custom_call_target="tpu_custom_call" | custom-call | tf_op jit(solution)/shard_map/pallas_call | solution.py:396
  137.0 0.8 copy.28
  (40 shorter events, 0.1 us)
Async XLA Ops:
  7.2 112.7 %copy-start = (bf16[1,512,2048]{2,1,0:T(8,128)(2,1)S(1)}, bf16[1,512,2048]{2,1,0:T(8,128)(2,1)}, u32[]{:S(2)}) copy-start(bf16[1,512,2048]{2,1,0:T(8,128)(2,1)} %param.23) | copy-start | bytes 6291460
  7.2 3.5 %copy-start.14 = (s32[64]{0:T(128)S(1)}, s32[64]{0:T(128)}, u32[]{:S(2)}) copy-start(s32[64]{0:T(128)} %param.19) | copy-start | bytes 772
  7.2 34.4 %all-gather.4.cloned.1.call-start = ((), (), s32[]{:S(2)}) async-start(), calls=%async_computation.1 | async-start | bytes 2621440 | tf_op jit(solution)/shard_map/all_gather | solution.py:427
  10.8 2.2 %copy-start.3 = (f32[8,8,128,128]{3,2,1,0:T(8,128)S(1)}, f32[8,8,128,128]{3,2,1,0:T(8,128)}, u32[]{:S(2)}) copy-start(f32[8,8,128,128]{3,2,1,0:T(8,128)} %cache_ref.1) | copy-start | bytes 12582916
  13.9 1.3 copy-start.1
  15.3 57.7 %all-to-all-start = ((bf16[8,8,128,128]{3,2,1,0:T(8,128)(2,1)}), bf16[8,8,128,128]{3,2,1,0:T(8,128)(2,1)}, u32[]{:S(2)}, u32[]{:S(2)}) async-start(bf16[8,8,128,128]{3,2,1,0:T(8,128)(2,1)} %copy-done.1), calls=%async_computation | async-start | bytes 4194304 | tf_op jit(solution)/shard_map/all_to_all | solution.py:437
  22.6 10.5 %copy-start.9 = (bf16[2048,4,256]{2,1,0:T(4,128)(2,1)S(1)}, bf16[2048,4,256]{2,1,0:T(4,128)(2,1)}, u32[]{:S(2)}) copy-start(bf16[2048,4,256]{2,1,0:T(4,128)(2,1)} %param.13) | copy-start | bytes 12582916
  33.1 3.1 %copy-start.10 = (bf16[2048,8,2]{0,2,1:T(2,128)(2,1)S(1)}, bf16[2048,8,2]{0,2,1:T(2,128)(2,1)}, u32[]{:S(2)}) copy-start(bf16[2048,8,2]{0,2,1:T(2,128)(2,1)} %param.15) | copy-start | bytes 196612
  33.1 3.1 %copy-start.13 = (f32[8]{0:T(128)S(1)}, f32[8]{0:T(128)}, u32[]{:S(2)}) copy-start(f32[8]{0:T(128)} %param.16) | copy-start | bytes 100
  33.1 3.3 %copy-start.11 = (f32[128,2]{0,1:T(2,128)S(1)}, f32[128,2]{0,1:T(2,128)}, u32[]{:S(2)}) copy-start(f32[128,2]{0,1:T(2,128)} %param.21) | copy-start | bytes 3076
  33.1 3.3 %copy-start.12 = (s32[128,2]{0,1:T(2,128)S(1)}, s32[128,2]{0,1:T(2,128)}, u32[]{:S(2)}) copy-start(s32[128,2]{0,1:T(2,128)} %param.20) | copy-start | bytes 3076
  41.6 25.6 %slice-start = ((s8[8388608]{0:T(1024)(128)(4,1)}), s8[4194304]{0:T(1024)(128)(4,1)S(1)}, s32[]{:S(2)}) async-start(s8[8388608]{0:T(1024)(128)(4,1)} %bitcast.25), calls=%async_computation.2 | async-start | bytes 8388608
  44.1 23.2 %slice-start.1 = ((s8[8388608]{0:T(1024)(128)(4,1)}), s8[4194304]{0:T(1024)(128)(4,1)S(1)}, s32[]{:S(2)}) async-start(s8[8388608]{0:T(1024)(128)(4,1)} %bitcast.25), calls=%async_computation.3 | async-start | bytes 8388608
  49.4 17.9 %copy-start.17 = (bf16[512,2048]{1,0:T(8,128)(2,1)S(1)}, bf16[512,2048]{1,0:T(8,128)(2,1)}, u32[]{:S(2)}) copy-start(bf16[512,2048]{1,0:T(8,128)(2,1)} %all-gather.4.cloned.1.call-done) | copy-start | bytes 6291460
  65.3 1.0 copy-start.5
  66.3 1.0 copy-start.7
  72.9 1.6 %copy-start.4 = (bf16[512,2048]{1,0:T(8,128)(2,1)S(1)}, bf16[512,2048]{1,0:T(8,128)(2,1)}, u32[]{:S(2)}) copy-start(bf16[512,2048]{1,0:T(8,128)(2,1)} %convolution_convert_fusion.1.vz_ref) | copy-start | bytes 6291460
  74.5 1.2 copy-start.6
  75.8 1.2 copy-start.8
  77.0 9.8 %copy-start.15 = (bf16[8,128,2048]{2,1,0:T(8,128)(2,1)S(1)}, bf16[8,128,2048]{2,1,0:T(8,128)(2,1)}, u32[]{:S(2)}) copy-start(bf16[8,128,2048]{2,1,0:T(8,128)(2,1)} %param.17) | copy-start | bytes 12582916
  86.8 2.4 %copy-start.2 = (bf16[128,2048]{1,0:T(8,128)(2,1)S(1)}, bf16[128,2048]{1,0:T(8,128)(2,1)}, u32[]{:S(2)}) copy-start(bf16[128,2048]{1,0:T(8,128)(2,1)} %tokens_ref.1) | copy-start | bytes 1572868
  86.8 30.7 %copy-start.16 = (bf16[1,2048,1024]{2,1,0:T(8,128)(2,1)S(1)}, bf16[1,2048,1024]{2,1,0:T(8,128)(2,1)}, u32[]{:S(2)}) copy-start(bf16[1,2048,1024]{2,1,0:T(8,128)(2,1)} %param.22) | copy-start | bytes 12582916
Sparse Core Ops, SparseCore 0:
  10.7 25.2 all-gather.3
